TPU v7x, 256 devices: a whole 4x4x8 slice. The times are simulated.
256 devices in a mesh: section: 32 (over x, y, z_lo), dp: 8 (over z_hi, core).
Axes of the slice: x: 4, y: 4, z: 8 (z_hi: 4, z_lo: 2; z = z_hi * 2 + z_lo), core: 2. Of those that a mesh axis runs over, the one named last changes fastest.
Arguments:
- pipe_maps: bfloat16 [32, 8, 8, 32, 384], P('section', 'dp'), may hold values from -6 to 6
- fresh_maps: bfloat16 [3, 8, 8, 32, 384], P(None, 'dp'), may hold values from -6 to 6
- teacher_weight: bfloat16 [64, 3, 3, 384, 384], P('section'), may hold values from -0.109375 to 0.109375
- student_depth: float32 [64, 49, 384], P('section'), may hold values from -0.875 to 0.875
- student_point: bfloat16 [64, 384, 384], P('section'), may hold values from -0.3125 to 0.3125
Outputs:
- final_maps: bfloat16 [32, 8, 8, 32, 384], P('section', 'dp')
- point_grad: float32 [64, 384, 384], P('section', None, 'dp')
- depth_grad: float32 [64, 49, 384], P('section', None, 'dp')
All inputs are finite; a program needn't handle non-finite values.
Results may differ from a plain program's by a relative error of at most 0.012.
Values may be sent and summed in bfloat16 or wider, within the bound.
No kernel may reach another device: no remote copies, remote signals or barrier semaphores. Data moves between devices by JAX's collectives and lax.ppermute only.
A program may use at most 128 MiB of HBM per device.

v0:
```python
import functools

import jax
import jax.numpy as jnp
import numpy as np
from jax import lax
from jax.experimental import pallas as pl
from jax.experimental.pallas import tpu as pltpu
from jax.sharding import PartitionSpec as P

ROWS, COLS, CHANS = 8, 32, 384
PIX = ROWS * COLS
TAPS = 49
LEN_Y, LEN_X = 11, 36
HALF = LEN_Y * LEN_X // 2
PART = 208
FREQ = 2 * PART
SLOT = 64
WIDE = 2 * CHANS + 2 * SLOT
CHIPS = 4
SHARE = CHANS // (2 * CHIPS)

F32, BF16 = jnp.float32, jnp.bfloat16
GELU_C = float(np.sqrt(2.0 / np.pi))
GELU_A = 0.044715


def transforms():
    wy = 2 * np.pi * np.arange(LEN_Y) / LEN_Y
    wx = 2 * np.pi * (np.arange(LEN_X // 2) + 0.5) / LEN_X
    wy, wx = (a.reshape(-1, 1) for a in np.meshgrid(wy, wx, indexing="ij"))
    y, x = (a.reshape(1, -1) for a in np.meshgrid(np.arange(ROWS), np.arange(COLS), indexing="ij"))
    ty, tx = (a.reshape(1, -1) - 3 for a in np.meshgrid(np.arange(7), np.arange(7), indexing="ij"))

    def stacked(top, bottom):
        gap = np.zeros((PART - HALF, top.shape[1]))
        return np.concatenate([top, gap, bottom, gap])

    pixel, tap = wy * y + wx * x, wy * ty + wx * tx
    forward = stacked(np.cos(pixel), -np.sin(pixel))
    taps = stacked(np.cos(tap), np.sin(tap))
    taps = np.pad(taps, ((0, 0), (0, SLOT - TAPS)))
    return forward, forward.T / HALF, taps


def side_shift(value, shift):
    col = lax.broadcasted_iota(jnp.int32, value.shape, 0) % COLS
    moved = pltpu.roll(value, shift % PIX, 0)
    keep = (col >= shift) if shift > 0 else (col < COLS + shift)
    return jnp.where(keep, moved, 0.0)


def fill_windows(win, value):
    win[COLS : COLS + PIX, 0:CHANS] = side_shift(value, 1).astype(BF16)
    win[COLS : COLS + PIX, CHANS : 2 * CHANS] = value.astype(BF16)
    win[COLS : COLS + PIX, 2 * CHANS :] = side_shift(value, -1).astype(BF16)


def teach_map(x, w, win, ready):
    edge = jnp.zeros((COLS, 3 * CHANS), BF16)
    win[0:COLS, :] = edge
    win[COLS + PIX :, :] = edge

    def conv(first):
        total = None
        for dy in range(3):
            ready(first + dy)
            part = jnp.dot(
                win[dy * COLS : dy * COLS + PIX, :], w[first + dy], preferred_element_type=F32
            )
            total = part if total is None else total + part
        return total

    fill_windows(win, x[...].astype(F32))
    fill_windows(win, jnp.maximum(conv(0), 0.0))
    summed = x[...].astype(F32) + conv(3)
    return (0.8 * summed).astype(BF16)


def first_teacher_kernel(x_ref, w_hbm, out_ref, w_ref, win, sem):
    copies = [pltpu.make_async_copy(w_hbm.at[i], w_ref.at[i], sem.at[i]) for i in range(6)]
    for copy in copies:
        copy.start()
    out_ref[...] = teach_map(x_ref, w_ref, win, lambda i: copies[i].wait())


def next_teacher_kernel(tick, moved_ref, fresh_ref, w_ref, after, out_ref, x_ref, win):
    leading = lax.axis_index("section") == 0

    @pl.when(leading)
    def _():
        x_ref[...] = fresh_ref[tick]

    @pl.when(jnp.logical_not(leading))
    def _():
        x_ref[...] = moved_ref[...]

    out_ref[...] = teach_map(x_ref, w_ref, win, lambda i: None)


VMEM = pl.BlockSpec(memory_space=pltpu.VMEM)
MAP = jax.ShapeDtypeStruct((PIX, CHANS), BF16)
WINDOWS = pltpu.VMEM((PIX + 2 * COLS, 3 * CHANS), BF16)
TEACHER_COST = pl.CostEstimate(
    flops=2 * 18 * PIX * CHANS * CHANS, bytes_accessed=2 * 18 * CHANS * CHANS, transcendentals=0
)


def first_teacher(x, weight):
    return pl.pallas_call(
        first_teacher_kernel,
        out_shape=[MAP, jax.ShapeDtypeStruct(weight.shape, BF16)],
        in_specs=[VMEM, pl.BlockSpec(memory_space=pltpu.HBM)],
        out_specs=[VMEM, VMEM],
        scratch_shapes=[WINDOWS, pltpu.SemaphoreType.DMA((6,))],
        compiler_params=pltpu.CompilerParams(vmem_limit_bytes=20 << 20),
        cost_estimate=TEACHER_COST,
        name="teacher",
    )(x, weight)


def next_teacher(tick, moved, fresh, weight, after):
    return pl.pallas_call(
        functools.partial(next_teacher_kernel, tick),
        out_shape=[MAP, MAP],
        in_specs=[VMEM, VMEM, VMEM, pl.BlockSpec(memory_space=pl.ANY)],
        out_specs=[VMEM, VMEM],
        scratch_shapes=[WINDOWS],
        compiler_params=pltpu.CompilerParams(vmem_limit_bytes=20 << 20),
        cost_estimate=TEACHER_COST,
        name="teacher",
    )(moved, fresh, weight, after)


def gelu_parts(act):
    t = jnp.tanh(GELU_C * (act + GELU_A * act * act * act))
    return t, 0.5 * (1.0 + t)


def gelu_slope(act, t):
    inner = GELU_C * (1.0 + 3.0 * GELU_A * act * act)
    return 0.5 * (1.0 + t) + 0.5 * act * (1.0 - t * t) * inner


CUTS = ((0, 256), (256, 384))


def student_kernel(first, last, *refs):
    refs = list(refs)
    x_ref, teach_ref, f_ref, g_ref, point_ref = refs[:5]
    del refs[:5]
    if first:
        tapf_ref, depth_ref = refs[:2]
        del refs[:2]
    else:
        spec_ref, pacc_in, zacc_in = refs[:3]
        del refs[:3]
        if last:
            tapf_ref = refs.pop(0)
    if last:
        keep_ref, give_ref, final_ref = refs[:3]
        out_ref, sem = refs[-2:]
        del refs[:3], refs[-2:]
        final = pltpu.make_async_copy(teach_ref, final_ref, sem)
        final.start()
    else:
        if first:
            spec_ref = refs.pop(0)
        pacc, zacc = refs[:2]
        del refs[:2]
    freq, dfreq, act, gel, u1, low = refs

    if first:
        for b in range(2):
            spec_ref[b] = jnp.dot(
                tapf_ref[:, 0:TAPS],
                depth_ref[:, b, :],
                preferred_element_type=F32,
                precision=lax.Precision.HIGHEST,
            )

    def halves(ref, lo, cut):
        rows = slice(lo, lo + 16)
        other = slice(PART + lo, PART + lo + 16)
        return ref[rows, cut], ref[other, cut]

    def transform(b, src, dst, cut):
        dst[b, :, cut] = jnp.dot(f_ref[...], src, preferred_element_type=F32)

    def back(cut, product):
        for lo in range(0, PART, 16):
            re, im = product(lo)
            low[lo : lo + 16, cut] = re.astype(BF16)
            low[PART + lo : PART + lo + 16, cut] = im.astype(BF16)
        return jnp.dot(g_ref[...], low[:, cut], preferred_element_type=F32)

    def times(lo, b, cut):
        ar, ai = halves(freq.at[b], lo, cut)
        kr, ki = halves(spec_ref.at[b], lo, cut)
        return ar * kr - ai * ki, ar * ki + ai * kr

    def times_conj(lo, b, cut):
        ar, ai = halves(dfreq.at[b], lo, cut)
        kr, ki = halves(spec_ref.at[b], lo, cut)
        return ar * kr + ai * ki, ai * kr - ar * ki

    def forward(b, src):
        for a, z in CUTS:
            cut = slice(a, z)
            transform(b, src[:, cut].astype(BF16), freq, cut)
            act[b, :, cut] = back(cut, lambda lo: times(lo, b, cut))
            for r in range(0, PIX, 32):
                rows = slice(r, r + 32)
                v = act[b, rows, cut]
                _, cdf = gelu_parts(v)
                gel[b, rows, cut] = (v * cdf).astype(BF16)
        return jnp.dot(gel[b], point_ref[b], preferred_element_type=F32)

    u1[...] = x_ref[...].astype(F32) + forward(0, x_ref)
    grad = (u1[...] + forward(1, u1) - teach_ref[...].astype(F32)) * (4.0 / PIX)
    u1[...] = grad

    for b in (1, 0):
        grad_low = u1[...].astype(BF16)
        part = lax.dot_general(
            grad_low, gel[b], (((0,), (0,)), ((), ())), preferred_element_type=F32
        )
        if not first:
            part = part + pacc_in[b]
        if last:
            out_ref[:, b * CHANS : (b + 1) * CHANS] = part.astype(BF16)
        else:
            pacc[b] = part
        for a, z in CUTS:
            cut = slice(a, z)
            dgel = lax.dot_general(
                grad_low, point_ref[b, cut], (((1,), (1,)), ((), ())), preferred_element_type=F32
            )
            v = act[b, :, cut]
            t, _ = gelu_parts(v)
            transform(b, (dgel * gelu_slope(v, t)).astype(BF16), dfreq, cut)
            if b == 1:
                u1[:, cut] = u1[:, cut] + back(cut, lambda lo: times_conj(lo, b, cut))
            for lo in range(0, PART, 16):
                ir, ii = halves(freq.at[b], lo, cut)
                dr, di = halves(dfreq.at[b], lo, cut)
                re, im = ir * dr + ii * di, ir * di - ii * dr
                if not first:
                    zr, zi = halves(zacc_in.at[b], lo, cut)
                    re, im = re + zr, im + zi
                if last:
                    low[lo : lo + 16, cut] = re.astype(BF16)
                    low[PART + lo : PART + lo + 16, cut] = im.astype(BF16)
                else:
                    zacc[b, lo : lo + 16, cut] = re
                    zacc[b, PART + lo : PART + lo + 16, cut] = im
        if last:
            taps = lax.dot_general(
                low[...], tapf_ref[...], (((0,), (0,)), ((), ())), preferred_element_type=F32
            )
            at = 2 * CHANS + b * SLOT
            out_ref[:, at : at + SLOT] = (taps * (1.0 / HALF)).astype(BF16)

    if last:
        core = lax.axis_index("dp") % 2
        for mine in range(2):

            @pl.when(core == mine)
            def _():
                for chip in range(keep_ref.shape[0]):
                    for target, ref in ((mine, keep_ref), (1 - mine, give_ref)):
                        at = (2 * chip + target) * SHARE
                        ref[chip] = out_ref[at : at + SHARE, :]

        final.wait()


def student(first, last, x, teach, consts, point, carried, extra):
    spec = jax.ShapeDtypeStruct((2, FREQ, CHANS), F32)
    pacc = jax.ShapeDtypeStruct((2, CHANS, CHANS), F32)
    args = [x, teach, *consts, point, *carried, *extra]
    if last:
        outs = [jax.ShapeDtypeStruct((CHIPS, SHARE, WIDE), BF16)] * 2 + [MAP]
    else:
        outs = ([spec] if first else []) + [pacc, spec]
    aliases = {} if first or last else {6: 0, 7: 1}
    return pl.pallas_call(
        functools.partial(student_kernel, first, last),
        out_shape=outs,
        in_specs=[VMEM] * len(args),
        out_specs=[VMEM, VMEM, pl.BlockSpec(memory_space=pl.ANY)] if last else [VMEM] * len(outs),
        input_output_aliases=aliases,
        scratch_shapes=[
            pltpu.VMEM((2, FREQ, CHANS), F32),
            pltpu.VMEM((2, FREQ, CHANS), F32),
            pltpu.VMEM((2, PIX, CHANS), F32),
            pltpu.VMEM((2, PIX, CHANS), BF16),
            pltpu.VMEM((PIX, CHANS), F32),
            pltpu.VMEM((FREQ, CHANS), BF16),
        ]
        + ([pltpu.VMEM((CHANS, WIDE), BF16), pltpu.SemaphoreType.DMA] if last else []),
        compiler_params=pltpu.CompilerParams(vmem_limit_bytes=32 << 20),
        cost_estimate=pl.CostEstimate(
            flops=2 * 13 * PIX * CHANS * CHANS,
            bytes_accessed=8 << 20,
            transcendentals=4 * PIX * CHANS,
        ),
        name="student",
    )(*args)


def fold_kernel(keep_ref, got_ref, mine_ref, *give_refs):
    chip = lax.axis_index("dp") // 2

    def block(index):
        return keep_ref[index].astype(F32) + got_ref[index].astype(F32)

    mine_ref[...] = block(chip)
    for ahead, ref in enumerate(give_refs, 1):
        ref[...] = block((chip + ahead) % CHIPS).astype(BF16)


def fold(keep, got):
    block = (SHARE, WIDE)
    return pl.pallas_call(
        fold_kernel,
        out_shape=[jax.ShapeDtypeStruct(block, F32)]
        + [jax.ShapeDtypeStruct(block, BF16)] * (CHIPS - 1),
        in_specs=[VMEM, VMEM],
        out_specs=[VMEM] * CHIPS,
        compiler_params=pltpu.CompilerParams(vmem_limit_bytes=8 << 20),
        name="fold_cores",
    )(keep, got)


def owner_kernel(mine_ref, *refs):
    *got_refs, point_ref, depth_ref = refs
    total = mine_ref[...]
    for ref in got_refs:
        total = total + ref[...].astype(F32)
    for b in range(2):
        point_ref[b] = total[:, b * CHANS : (b + 1) * CHANS]
        at = 2 * CHANS + b * SLOT
        depth_ref[b] = total[:, at : at + TAPS]


def owner(mine, got):
    return pl.pallas_call(
        owner_kernel,
        out_shape=[
            jax.ShapeDtypeStruct((2, SHARE, CHANS), F32),
            jax.ShapeDtypeStruct((2, SHARE, TAPS), F32),
        ],
        in_specs=[VMEM] * CHIPS,
        out_specs=[VMEM, VMEM],
        compiler_params=pltpu.CompilerParams(vmem_limit_bytes=8 << 20),
        name="owner_sum",
    )(mine, *got)


def sum_at_owner(keep, give):
    devices = 2 * CHIPS
    got = lax.ppermute(give, "dp", [(i, i ^ 1) for i in range(devices)])
    mine, *gives = fold(keep, got)
    routes = [[(i, (i + 2 * ahead) % devices) for i in range(devices)] for ahead in (1, 2, 3)]
    got = [lax.ppermute(block, "dp", route) for block, route in zip(gives, routes)]
    point, depth = owner(mine, got)
    return jnp.swapaxes(point, 1, 2), jnp.swapaxes(depth, 1, 2)


def from_behind(block, axis, distance):
    devices = range(lax.axis_size(axis))
    route = [(i - distance, i) for i in devices if i - distance in devices]
    return lax.ppermute(block, axis, route)


def body(pipe_maps, fresh_maps, teacher_weight, student_depth, student_point):
    ticks = fresh_maps.shape[0] + 1
    weight = teacher_weight.reshape(6, 3 * CHANS, CHANS)
    weight = pltpu.with_memory_space_constraint(weight, pltpu.HBM)
    fresh = fresh_maps.reshape(ticks - 1, PIX, CHANS)
    depth = jnp.swapaxes(student_depth, 0, 1)
    forward, inverse, taps = transforms()
    consts = (jnp.asarray(forward, BF16), jnp.asarray(inverse, BF16))
    current = pipe_maps.reshape(PIX, CHANS)
    carried, extra = (), (jnp.asarray(taps, F32), depth)
    for tick in range(ticks):
        first, last = tick == 0, tick == ticks - 1
        if first:
            teach, weight = first_teacher(current, weight)
        else:
            teach, current = next_teacher(tick - 1, moved, fresh, weight, carried[1])
        if not last:
            moved = from_behind(teach, "section", 1)
        if last:
            extra = (jnp.asarray(taps, BF16),)
        result = student(first, last, current, teach, consts, student_point, carried, extra)
        if first:
            spectrum = result[0]
            carried, extra = tuple(result), ()
        else:
            carried = (spectrum, *result)
    keep, give, final = result
    point_total, depth_total = sum_at_owner(keep, give)
    return (final.reshape(1, 1, ROWS, COLS, CHANS), point_total, depth_total)


def solution(mesh):
    placed = (
        P("section", "dp", None, None, None),
        P(None, "dp", None, None, None),
        P("section", None, None, None, None),
        P("section", None, None),
        P("section", None, None),
    )
    return jax.shard_map(
        body,
        mesh=mesh,
        in_specs=placed,
        out_specs=(
            P("section", "dp", None, None, None),
            P("section", None, "dp"),
            P("section", None, "dp"),
        ),
        check_vma=False,
    )
```

profile of v0, /device:TPU:6, one launch (start us, length us, event | category | flops | bytes accessed | tf_op | source)
XLA Modules:
  0.0 67.7 jit_solution(11722515161454582212)
XLA Ops:
  0.6 0.0 copy-start.4
  0.6 0.9 %copy-done.4 = bf16[1,1,8,32,384]{4,3,2,1,0:T(8,128)(2,1)S(1)} copy-done((bf16[1,1,8,32,384]{4,3,2,1,0:T(8,128)(2,1)S(1)}, bf16[1,1,8,32,384]{4,3,2,1,0:T(8,128)(2,1)}, u32[]{:S(2)}) %copy-start.4) | copy-done | bytes 196632
  1.6 0.0 copy-start.1
  1.6 0.0 copy-start.2
  1.6 0.0 copy-start.3
  1.6 0.0 copy-start.5
  1.6 0.0 copy-start.7
  1.6 0.0 copy-start.8
  1.6 4.5 %teacher.4 = (bf16[256,384]{1,0:T(8,128)(2,1)S(1)}, bf16[6,1152,384]{2,1,0:T(8,128)(2,1)S(1)}) custom-call(bf16[256,384]{1,0:T(8,128)(2,1)S(1)} %bitcast.10, bf16[6,1152,384]{2,1,0:T(8,128)(2,1)} %bitcast.13), custom_call_target="tpu_custom_call" | custom-call | flops 1358954496 | bytes 5308416 | tf_op jit(solution)/shard_map/teacher/pallas_call | solution.py:110
  6.1 3.8 %collective-permute-start = (bf16[256,384]{1,0:T(8,128)(2,1)S(1)}, bf16[256,384]{1,0:T(8,128)(2,1)S(1)}, u32[]{:S(2)}, u32[]{:S(2)}) collective-permute-start(bf16[256,384]{1,0:T(8,128)(2,1)S(1)} %get-tuple-element.27.refs_1_), channel_id=1, source_target_pairs={{0,8},{8,16},{16,24},{24,32},{32,40},{40,48},{48,56},{56,64},{64,7... | collective-permute-start | bytes 589832 | tf_op jit(solution)/shard_map/ppermute | solution.py:374
  9.9 0.0 copy-done.1
  9.9 0.0 copy-done.2
  9.9 0.0 copy-done.3
  9.9 0.0 copy-done.5
  9.9 0.0 copy-done.7
  9.9 0.0 copy-done.8
  9.9 0.0 copy-start
  10.0 4.8 %student.4 = (f32[2,416,384]{2,1,0:T(8,128)S(1)}, f32[2,384,384]{2,1,0:T(8,128)S(1)}, f32[2,416,384]{2,1,0:T(8,128)S(1)}) custom-call(bf16[256,384]{1,0:T(8,128)(2,1)S(1)} %bitcast.11, bf16[256,384]{1,0:T(8,128)(2,1)S(1)} %get-tuple-element.27.refs_1_, bf16[416,256]{1,0:T(8,128)(2,1)S(1)} %copy-done.3, bf16[256,416]{1,0:T(8,128)(2,1)S(1)} %copy-done.2, ...), custom_call_target="tpu_custom_call" | custom-call | flops 981467136 | bytes 8388608 | tf_op jit(solution)/shard_map/student/pallas_call | solution.py:287
  14.8 2.8 %collective-permute-done.moved_ref = bf16[256,384]{1,0:T(8,128)(2,1)S(1)} collective-permute-done((bf16[256,384]{1,0:T(8,128)(2,1)S(1)}, bf16[256,384]{1,0:T(8,128)(2,1)S(1)}, u32[]{:S(2)}, u32[]{:S(2)}) %collective-permute-start) | collective-permute-done | bytes 196640 | tf_op jit(solution)/shard_map/ppermute | solution.py:374
  17.6 0.0 copy-done
  17.6 2.6 %teacher.5 = (bf16[256,384]{1,0:T(8,128)(2,1)S(1)}, bf16[256,384]{1,0:T(8,128)(2,1)S(1)}) custom-call(bf16[256,384]{1,0:T(8,128)(2,1)S(1)} %collective-permute-done.moved_ref, bf16[3,256,384]{2,1,0:T(8,128)(2,1)S(1)} %bitcast.7, bf16[6,1152,384]{2,1,0:T(8,128)(2,1)S(1)} %get-tuple-element.28.w_ref, f32[2,384,384]{2,1,0:T(8,128)S(1)} %get-tuple-element.29.after.refs_6_), custom_call_target="tpu_custom_call" | custom-call | flops 1358954496 | bytes 5308416 | tf_op jit(solution)/shard_map/teacher/pallas_call | solution.py:123
  20.2 2.1 %collective-permute-start.1 = (bf16[256,384]{1,0:T(8,128)(2,1)S(1)}, bf16[256,384]{1,0:T(8,128)(2,1)S(1)}, u32[]{:S(2)}, u32[]{:S(2)}) collective-permute-start(bf16[256,384]{1,0:T(8,128)(2,1)S(1)} %get-tuple-element.30.refs_1_), channel_id=1, source_target_pairs={{0,8},{8,16},{16,24},{24,32},{32,40},{40,48},{48,56},{56,64},{64,7... | collective-permute-start | bytes 589832 | tf_op jit(solution)/shard_map/ppermute | solution.py:374
  22.3 4.1 %student.5 = (f32[2,384,384]{2,1,0:T(8,128)S(1)}, f32[2,416,384]{2,1,0:T(8,128)S(1)}) custom-call(bf16[256,384]{1,0:T(8,128)(2,1)S(1)} %get-tuple-element.31.refs_0_, bf16[256,384]{1,0:T(8,128)(2,1)S(1)} %get-tuple-element.30.refs_1_, bf16[416,256]{1,0:T(8,128)(2,1)S(1)} %copy-done.3, ...), custom_call_target="tpu_custom_call", output_to_operand_aliasing={{0}: (6, {}), {1}: (7, {})} | custom-call | flops 981467136 | bytes 8388608 | tf_op jit(solution)/shard_map/student/pallas_call | solution.py:287
  26.4 4.5 %collective-permute-done.1.moved_ref = bf16[256,384]{1,0:T(8,128)(2,1)S(1)} collective-permute-done((bf16[256,384]{1,0:T(8,128)(2,1)S(1)}, bf16[256,384]{1,0:T(8,128)(2,1)S(1)}, u32[]{:S(2)}, u32[]{:S(2)}) %collective-permute-start.1) | collective-permute-done | bytes 196640 | tf_op jit(solution)/shard_map/ppermute | solution.py:374
  30.9 2.6 %teacher.6 = (bf16[256,384]{1,0:T(8,128)(2,1)S(1)}, bf16[256,384]{1,0:T(8,128)(2,1)S(1)}) custom-call(bf16[256,384]{1,0:T(8,128)(2,1)S(1)} %collective-permute-done.1.moved_ref, bf16[3,256,384]{2,1,0:T(8,128)(2,1)S(1)} %bitcast.8, bf16[6,1152,384]{2,1,0:T(8,128)(2,1)S(1)} %get-tuple-element.28.w_ref, f32[2,384,384]{2,1,0:T(8,128)S(1)} %get-tuple-element.34.after.refs_6_), custom_call_target="tpu_custom_call" | custom-call | flops 1358954496 | bytes 5308416 | tf_op jit(solution)/shard_map/teacher/pallas_call | solution.py:123
  33.5 1.9 %collective-permute-start.2 = (bf16[256,384]{1,0:T(8,128)(2,1)S(1)}, bf16[256,384]{1,0:T(8,128)(2,1)S(1)}, u32[]{:S(2)}, u32[]{:S(2)}) collective-permute-start(bf16[256,384]{1,0:T(8,128)(2,1)S(1)} %get-tuple-element.35.refs_1_), channel_id=1, source_target_pairs={{0,8},{8,16},{16,24},{24,32},{32,40},{40,48},{48,56},{56,64},{64,7... | collective-permute-start | bytes 589832 | tf_op jit(solution)/shard_map/ppermute | solution.py:374
  35.4 4.1 %student.6 = (f32[2,384,384]{2,1,0:T(8,128)S(1)}, f32[2,416,384]{2,1,0:T(8,128)S(1)}) custom-call(bf16[256,384]{1,0:T(8,128)(2,1)S(1)} %get-tuple-element.36.refs_0_, bf16[256,384]{1,0:T(8,128)(2,1)S(1)} %get-tuple-element.35.refs_1_, bf16[416,256]{1,0:T(8,128)(2,1)S(1)} %copy-done.3, ...), custom_call_target="tpu_custom_call", output_to_operand_aliasing={{0}: (6, {}), {1}: (7, {})} | custom-call | flops 981467136 | bytes 8388608 | tf_op jit(solution)/shard_map/student/pallas_call | solution.py:287
  39.5 4.6 %collective-permute-done.2.moved_ref = bf16[256,384]{1,0:T(8,128)(2,1)S(1)} collective-permute-done((bf16[256,384]{1,0:T(8,128)(2,1)S(1)}, bf16[256,384]{1,0:T(8,128)(2,1)S(1)}, u32[]{:S(2)}, u32[]{:S(2)}) %collective-permute-start.2) | collective-permute-done | bytes 196640 | tf_op jit(solution)/shard_map/ppermute | solution.py:374
  44.1 0.0 copy-start.6
  44.1 2.8 %teacher.7 = (bf16[256,384]{1,0:T(8,128)(2,1)S(1)}, bf16[256,384]{1,0:T(8,128)(2,1)S(1)}) custom-call(bf16[256,384]{1,0:T(8,128)(2,1)S(1)} %collective-permute-done.2.moved_ref, bf16[3,256,384]{2,1,0:T(8,128)(2,1)S(1)} %bitcast.9, bf16[6,1152,384]{2,1,0:T(8,128)(2,1)S(1)} %get-tuple-element.28.w_ref, f32[2,384,384]{2,1,0:T(8,128)S(1)} %get-tuple-element.38.after.refs_6_), custom_call_target="tpu_custom_call" | custom-call | flops 1358954496 | bytes 5308416 | tf_op jit(solution)/shard_map/teacher/pallas_call | solution.py:123
  46.9 0.0 copy-done.6
  46.9 4.0 %student.7 = (bf16[4,48,896]{2,1,0:T(8,128)(2,1)S(1)}, bf16[4,48,896]{2,1,0:T(8,128)(2,1)S(1)}, bf16[256,384]{1,0:T(8,128)(2,1)}) custom-call(bf16[256,384]{1,0:T(8,128)(2,1)S(1)} %get-tuple-element.39.refs_0_, bf16[256,384]{1,0:T(8,128)(2,1)S(1)} %get-tuple-element.40.refs_1_, bf16[416,256]{1,0:T(8,128)(2,1)S(1)} %copy-done.3, ...), custom_call_target="tpu_custom_call" | custom-call | flops 981467136 | bytes 8388608 | tf_op jit(solution)/shard_map/student/pallas_call | solution.py:287
  51.0 0.1 collective-permute-start.3
  51.1 1.6 %collective-permute-done.3.got_ref = bf16[4,48,896]{2,1,0:T(8,128)(2,1)S(1)} collective-permute-done((bf16[4,48,896]{2,1,0:T(8,128)(2,1)S(1)}, bf16[4,48,896]{2,1,0:T(8,128)(2,1)S(1)}, u32[]{:S(2)}, u32[]{:S(2)}) %collective-permute-start.3) | collective-permute-done | bytes 344096 | tf_op jit(solution)/shard_map/ppermute | solution.py:363
  52.7 0.1 fold_cores.1
  52.8 3.4 %collective-permute-start.4 = (bf16[48,896]{1,0:T(8,128)(2,1)S(1)}, bf16[48,896]{1,0:T(8,128)(2,1)S(1)}, u32[]{:S(2)}, u32[]{:S(2)}) collective-permute-start(bf16[48,896]{1,0:T(8,128)(2,1)S(1)} %get-tuple-element.46), channel_id=1, source_target_pairs={{0,2},{1,3},{2,4},{3,5},{4,6},{5,7},{6,0},{7,1},{8,10},{9,11},{10,... | collective-permute-start | bytes 258056 | tf_op jit(solution)/shard_map/ppermute | solution.py:366
  56.2 5.4 %collective-permute-start.5 = (bf16[48,896]{1,0:T(8,128)(2,1)S(1)}, bf16[48,896]{1,0:T(8,128)(2,1)S(1)}, u32[]{:S(2)}, u32[]{:S(2)}) collective-permute-start(bf16[48,896]{1,0:T(8,128)(2,1)S(1)} %get-tuple-element.47), channel_id=1, source_target_pairs={{0,4},{1,5},{2,6},{3,7},{4,0},{5,1},{6,2},{7,3},{8,12},{9,13},{10,... | collective-permute-start | bytes 258056 | tf_op jit(solution)/shard_map/ppermute | solution.py:366
  61.6 2.6 %collective-permute-start.6 = (bf16[48,896]{1,0:T(8,128)(2,1)S(1)}, bf16[48,896]{1,0:T(8,128)(2,1)S(1)}, u32[]{:S(2)}, u32[]{:S(2)}) collective-permute-start(bf16[48,896]{1,0:T(8,128)(2,1)S(1)} %get-tuple-element.48), channel_id=1, source_target_pairs={{0,6},{1,7},{2,0},{3,1},{4,2},{5,3},{6,4},{7,5},{8,14},{9,15},{10,... | collective-permute-start | bytes 258056 | tf_op jit(solution)/shard_map/ppermute | solution.py:366
  64.2 0.0 collective-permute-done.4.refs_0_
  64.2 2.3 %collective-permute-done.5.refs_1_ = bf16[48,896]{1,0:T(8,128)(2,1)S(1)} collective-permute-done((bf16[48,896]{1,0:T(8,128)(2,1)S(1)}, bf16[48,896]{1,0:T(8,128)(2,1)S(1)}, u32[]{:S(2)}, u32[]{:S(2)}) %collective-permute-start.5) | collective-permute-done | bytes 86048 | tf_op jit(solution)/shard_map/ppermute | solution.py:366
  66.5 0.4 collective-permute-done.6.refs_2_
  66.9 0.7 %owner_sum.1 = (f32[2,48,384]{2,1,0:T(8,128)}, f32[2,48,49]{2,1,0:T(8,128)}) custom-call(f32[48,896]{1,0:T(8,128)S(1)} %get-tuple-element.45.mine_ref, bf16[48,896]{1,0:T(8,128)(2,1)S(1)} %collective-permute-done.4.refs_0_, bf16[48,896]{1,0:T(8,128)(2,1)S(1)} %collective-permute-done.5.refs_1_, bf16[48,896]{1,0:T(8,128)(2,1)S(1)} %collective-permute-done.6.refs_2_), custom_call_target="tpu_custom_call" | custom-call | tf_op jit(solution)/shard_map/owner_sum/pallas_call | solution.py:348
Async XLA Ops:
  0.6 0.9 %copy-start.4 = (bf16[1,1,8,32,384]{4,3,2,1,0:T(8,128)(2,1)S(1)}, bf16[1,1,8,32,384]{4,3,2,1,0:T(8,128)(2,1)}, u32[]{:S(2)}) copy-start(bf16[1,1,8,32,384]{4,3,2,1,0:T(8,128)(2,1)} %param.9) | copy-start | bytes 589828
  1.6 8.3 %copy-start.1 = (bf16[2,384,384]{2,1,0:T(8,128)(2,1)S(1)}, bf16[2,384,384]{2,1,0:T(8,128)(2,1)}, u32[]{:S(2)}) copy-start(bf16[2,384,384]{2,1,0:T(8,128)(2,1)} %refs_4_.7) | copy-start | bytes 1769476
  1.6 8.3 %copy-start.2 = (bf16[256,416]{1,0:T(8,128)(2,1)S(1)}, bf16[256,416]{1,0:T(8,128)(2,1)}, u32[]{:S(2)}) copy-start(bf16[256,416]{1,0:T(8,128)(2,1)} %constant.9.clone.refs_3_) | copy-start | bytes 638980
  1.6 8.3 %copy-start.3 = (bf16[416,256]{1,0:T(8,128)(2,1)S(1)}, bf16[416,256]{1,0:T(8,128)(2,1)}, u32[]{:S(2)}) copy-start(bf16[416,256]{1,0:T(8,128)(2,1)} %constant.8.clone.refs_2_) | copy-start | bytes 638980
  1.6 8.4 %copy-start.5 = (bf16[1,1,8,32,384]{4,3,2,1,0:T(8,128)(2,1)S(1)}, bf16[1,1,8,32,384]{4,3,2,1,0:T(8,128)(2,1)}, u32[]{:S(2)}) copy-start(bf16[1,1,8,32,384]{4,3,2,1,0:T(8,128)(2,1)} %param.9) | copy-start | bytes 589828
  1.6 8.4 %copy-start.7 = (f32[2,49,384]{2,0,1:T(2,128)S(1)}, f32[2,49,384]{2,0,1:T(2,128)}, u32[]{:S(2)}) copy-start(f32[2,49,384]{2,0,1:T(2,128)} %param.12) | copy-start | bytes 451588
  1.6 8.4 %copy-start.8 = (f32[416,64]{1,0:T(8,128)S(1)}, f32[416,64]{1,0:T(8,128)}, u32[]{:S(2)}) copy-start(f32[416,64]{1,0:T(8,128)} %constant.10.clone.refs_5_) | copy-start | bytes 319492
  6.1 11.5 %collective-permute-start = (bf16[256,384]{1,0:T(8,128)(2,1)S(1)}, bf16[256,384]{1,0:T(8,128)(2,1)S(1)}, u32[]{:S(2)}, u32[]{:S(2)}) collective-permute-start(bf16[256,384]{1,0:T(8,128)(2,1)S(1)} %get-tuple-element.27.refs_1_), channel_id=1, source_target_pairs={{0,8},{8,16},{16,24},{24,32},{32,40},{40,48},{48,56},{56,64},{64,7... | collective-permute-start | bytes 589832 | tf_op jit(solution)/shard_map/ppermute | solution.py:374
  9.9 7.7 %copy-start = (bf16[3,1,8,32,384]{4,3,2,1,0:T(8,128)(2,1)S(1)}, bf16[3,1,8,32,384]{4,3,2,1,0:T(8,128)(2,1)}, u32[]{:S(2)}) copy-start(bf16[3,1,8,32,384]{4,3,2,1,0:T(8,128)(2,1)} %param.10) | copy-start | bytes 1769476
  20.2 10.7 %collective-permute-start.1 = (bf16[256,384]{1,0:T(8,128)(2,1)S(1)}, bf16[256,384]{1,0:T(8,128)(2,1)S(1)}, u32[]{:S(2)}, u32[]{:S(2)}) collective-permute-start(bf16[256,384]{1,0:T(8,128)(2,1)S(1)} %get-tuple-element.30.refs_1_), channel_id=1, source_target_pairs={{0,8},{8,16},{16,24},{24,32},{32,40},{40,48},{48,56},{56,64},{64,7... | collective-permute-start | bytes 589832 | tf_op jit(solution)/shard_map/ppermute | solution.py:374
  33.5 10.6 %collective-permute-start.2 = (bf16[256,384]{1,0:T(8,128)(2,1)S(1)}, bf16[256,384]{1,0:T(8,128)(2,1)S(1)}, u32[]{:S(2)}, u32[]{:S(2)}) collective-permute-start(bf16[256,384]{1,0:T(8,128)(2,1)S(1)} %get-tuple-element.35.refs_1_), channel_id=1, source_target_pairs={{0,8},{8,16},{16,24},{24,32},{32,40},{40,48},{48,56},{56,64},{64,7... | collective-permute-start | bytes 589832 | tf_op jit(solution)/shard_map/ppermute | solution.py:374
  44.1 2.8 %copy-start.6 = (bf16[416,64]{1,0:T(8,128)(2,1)S(1)}, bf16[416,64]{1,0:T(8,128)(2,1)}, u32[]{:S(2)}) copy-start(bf16[416,64]{1,0:T(8,128)(2,1)} %constant.11.clone.refs_8_) | copy-start | bytes 159748
  51.0 1.7 %collective-permute-start.3 = (bf16[4,48,896]{2,1,0:T(8,128)(2,1)S(1)}, bf16[4,48,896]{2,1,0:T(8,128)(2,1)S(1)}, u32[]{:S(2)}, u32[]{:S(2)}) collective-permute-start(bf16[4,48,896]{2,1,0:T(8,128)(2,1)S(1)} %get-tuple-element.44), channel_id=1, source_target_pairs={{0,1},{1,0},{2,3},{3,2},{4,5},{5,4},{6,7},{7,6},{8,9},{9,8},{10,11... | collective-permute-start | bytes 1032200 | tf_op jit(solution)/shard_map/ppermute | solution.py:363
  52.8 11.4 %collective-permute-start.4 = (bf16[48,896]{1,0:T(8,128)(2,1)S(1)}, bf16[48,896]{1,0:T(8,128)(2,1)S(1)}, u32[]{:S(2)}, u32[]{:S(2)}) collective-permute-start(bf16[48,896]{1,0:T(8,128)(2,1)S(1)} %get-tuple-element.46), channel_id=1, source_target_pairs={{0,2},{1,3},{2,4},{3,5},{4,6},{5,7},{6,0},{7,1},{8,10},{9,11},{10,... | collective-permute-start | bytes 258056 | tf_op jit(solution)/shard_map/ppermute | solution.py:366
  56.2 10.4 %collective-permute-start.5 = (bf16[48,896]{1,0:T(8,128)(2,1)S(1)}, bf16[48,896]{1,0:T(8,128)(2,1)S(1)}, u32[]{:S(2)}, u32[]{:S(2)}) collective-permute-start(bf16[48,896]{1,0:T(8,128)(2,1)S(1)} %get-tuple-element.47), channel_id=1, source_target_pairs={{0,4},{1,5},{2,6},{3,7},{4,0},{5,1},{6,2},{7,3},{8,12},{9,13},{10,... | collective-permute-start | bytes 258056 | tf_op jit(solution)/shard_map/ppermute | solution.py:366
  61.6 5.4 %collective-permute-start.6 = (bf16[48,896]{1,0:T(8,128)(2,1)S(1)}, bf16[48,896]{1,0:T(8,128)(2,1)S(1)}, u32[]{:S(2)}, u32[]{:S(2)}) collective-permute-start(bf16[48,896]{1,0:T(8,128)(2,1)S(1)} %get-tuple-element.48), channel_id=1, source_target_pairs={{0,6},{1,7},{2,0},{3,1},{4,2},{5,3},{6,4},{7,5},{8,14},{9,15},{10,... | collective-permute-start | bytes 258056 | tf_op jit(solution)/shard_map/ppermute | solution.py:366
where the time goes:
time: 67.8 us; the launch traced here: 67.7 us
  Pallas kernels  30.3 us (45%)
  starting transfers between devices  19.3 us (28%)
  waiting for transfers between devices  16.3 us (24%)
  local copies, waits for them, and re-layouts  0.96 us (1%)
  between operations  0.83 us (1%)
    pallas_call x4, Pallas kernels, student(): pl.pallas_call(functools.partial(student_kernel, first, last), out_shape=...  17 us
    ppermute x3, waiting for transfers between devices, from_behind(): return lax.ppermute(block, axis, route)  11.9 us
    ppermute x3, starting transfers between devices, sum_at_owner(): lax.ppermute(block, 'dp', route)  11.4 us
    pallas_call x3, Pallas kernels, next_teacher(): pl.pallas_call(functools.partial(next_teacher_kernel, tick), out_shape=[M...  8.05 us
    ppermute x3, starting transfers between devices, from_behind(): return lax.ppermute(block, axis, route)  7.85 us
    pallas_call x1, Pallas kernels, first_teacher(): pl.pallas_call(first_teacher_kernel, out_shape=[MAP, jax.ShapeDtypeStruct...  4.45 us
    ppermute x3, waiting for transfers between devices, sum_at_owner(): lax.ppermute(block, 'dp', route)  2.76 us
    ppermute x1, waiting for transfers between devices, sum_at_owner(): got = lax.ppermute(give, 'dp', [(i, i ^ 1) for i in range(devices)])  1.64 us
  transfers between devices with their start and end apart: 7, of which 6 were waited for; matrix products, arithmetic and copies ran while one was open for 0% of the time, Pallas kernels for 19%

commit v1 on v0

--- a/solution.py
+++ b/solution.py
@@ -77,25 +77,77 @@
     return (0.8 * summed).astype(BF16)
 
 
-def first_teacher_kernel(x_ref, w_hbm, out_ref, w_ref, win, sem):
-    copies = [pltpu.make_async_copy(w_hbm.at[i], w_ref.at[i], sem.at[i]) for i in range(6)]
-    for copy in copies:
-        copy.start()
-    out_ref[...] = teach_map(x_ref, w_ref, win, lambda i: copies[i].wait())
-
-
-def next_teacher_kernel(tick, moved_ref, fresh_ref, w_ref, after, out_ref, x_ref, win):
-    leading = lax.axis_index("section") == 0
-
-    @pl.when(leading)
+FLIGHT = 2
+MORE = 2
+
+
+def first_teacher_kernel(x_hbm, w_hbm, *refs):
+    others = len(refs) // 2 - 3
+    out_ref, w_ref, x_ref = refs[others : others + 3]
+    win, sem, x_sem = refs[-3:]
+    load = pltpu.make_async_copy(x_hbm, x_ref, x_sem)
+    load.start()
+    pairs = [(w_hbm.at[i], w_ref.at[i]) for i in range(6)]
+    pairs += zip(refs[:others], refs[others + 3 : -3])
+    copies = [pltpu.make_async_copy(*pair, sem.at[i]) for i, pair in enumerate(pairs)]
+    waiting = list(copies)
+
+    def start(count):
+        for copy in waiting[:count]:
+            copy.start()
+        del waiting[:count]
+
+    def ready(i):
+        copies[i].wait()
+        start(MORE)
+
+    start(FLIGHT)
+    load.wait()
+    out_ref[...] = teach_map(x_ref, w_ref, win, ready)
+    start(len(waiting))
+    for copy in copies[6:]:
+        copy.wait()
+
+
+def take_input(tick, refs, fresh_ref, x_ref):
+    section = lax.axis_index("section")
+
+    @pl.when(section == 0)
     def _():
         x_ref[...] = fresh_ref[tick]
 
-    @pl.when(jnp.logical_not(leading))
+    for parity, ref in enumerate(refs):
+
+        @pl.when(jnp.logical_and(section != 0, section % len(refs) == len(refs) - 1 - parity))
+        def _():
+            x_ref[...] = ref[...]
+
+
+def whole_teacher_kernel(tick, fresh_ref, w_ref, after, *refs):
+    *moved, out_ref, x_ref, win = refs
+    take_input(tick, moved, fresh_ref, x_ref)
+    out_ref[...] = teach_map(x_ref, w_ref, win, lambda i: None)
+
+
+def odd_teacher_kernel(tick, fresh_ref, w_ref, after, *refs):
+    *moved, out_ref, x_ref, win = refs
+    take_input(tick, moved, fresh_ref, x_ref)
+
+    @pl.when(lax.axis_index("section") % 2 == 1)
     def _():
-        x_ref[...] = moved_ref[...]
-
-    out_ref[...] = teach_map(x_ref, w_ref, win, lambda i: None)
+        out_ref[...] = teach_map(x_ref, w_ref, win, lambda i: None)
+
+
+def even_teacher_kernel(x_ref, w_ref, odd_ref, out_ref, win):
+    even = lax.axis_index("section") % 2 == 0
+
+    @pl.when(even)
+    def _():
+        out_ref[...] = teach_map(x_ref, w_ref, win, lambda i: None)
+
+    @pl.when(jnp.logical_not(even))
+    def _():
+        out_ref[...] = odd_ref[...]
 
 
 VMEM = pl.BlockSpec(memory_space=pltpu.VMEM)
@@ -106,43 +158,75 @@
 )
 
 
-def first_teacher(x, weight):
+def first_teacher(x, weight, *others):
+    held = [jax.ShapeDtypeStruct(a.shape, a.dtype) for a in (weight, x, *others)]
+    args = [pltpu.with_memory_space_constraint(a, pltpu.HBM) for a in (x, weight, *others)]
     return pl.pallas_call(
         first_teacher_kernel,
-        out_shape=[MAP, jax.ShapeDtypeStruct(weight.shape, BF16)],
-        in_specs=[VMEM, pl.BlockSpec(memory_space=pltpu.HBM)],
-        out_specs=[VMEM, VMEM],
-        scratch_shapes=[WINDOWS, pltpu.SemaphoreType.DMA((6,))],
+        out_shape=[MAP, *held],
+        in_specs=[pl.BlockSpec(memory_space=pltpu.HBM)] * len(args),
+        out_specs=[VMEM] * (1 + len(held)),
+        scratch_shapes=[
+            WINDOWS,
+            pltpu.SemaphoreType.DMA((6 + len(others),)),
+            pltpu.SemaphoreType.DMA,
+        ],
         compiler_params=pltpu.CompilerParams(vmem_limit_bytes=20 << 20),
         cost_estimate=TEACHER_COST,
         name="teacher",
-    )(x, weight)
-
-
-def next_teacher(tick, moved, fresh, weight, after):
-    return pl.pallas_call(
-        functools.partial(next_teacher_kernel, tick),
+    )(*args)
+
+
+def next_teacher(kernel, tick, moved, fresh, weight, after):
+    return pl.pallas_call(
+        functools.partial(kernel, tick),
         out_shape=[MAP, MAP],
-        in_specs=[VMEM, VMEM, VMEM, pl.BlockSpec(memory_space=pl.ANY)],
+        in_specs=[VMEM, VMEM, pl.BlockSpec(memory_space=pl.ANY)] + [VMEM] * len(moved),
         out_specs=[VMEM, VMEM],
         scratch_shapes=[WINDOWS],
         compiler_params=pltpu.CompilerParams(vmem_limit_bytes=20 << 20),
         cost_estimate=TEACHER_COST,
         name="teacher",
-    )(moved, fresh, weight, after)
-
-
-def gelu_parts(act):
-    t = jnp.tanh(GELU_C * (act + GELU_A * act * act * act))
-    return t, 0.5 * (1.0 + t)
-
-
-def gelu_slope(act, t):
-    inner = GELU_C * (1.0 + 3.0 * GELU_A * act * act)
-    return 0.5 * (1.0 + t) + 0.5 * act * (1.0 - t * t) * inner
-
-
-CUTS = ((0, 256), (256, 384))
+    )(fresh, weight, after, *moved)
+
+
+def even_teacher(x, weight, odd):
+    return pl.pallas_call(
+        even_teacher_kernel,
+        out_shape=MAP,
+        in_specs=[VMEM] * 3,
+        out_specs=VMEM,
+        scratch_shapes=[WINDOWS],
+        compiler_params=pltpu.CompilerParams(vmem_limit_bytes=20 << 20),
+        cost_estimate=TEACHER_COST,
+        name="teacher_even",
+    )(x, weight, odd)
+
+
+def settled_kernel(x_ref, out_ref):
+    out_ref[...] = x_ref[...]
+
+
+def settled(x):
+    return pl.pallas_call(
+        settled_kernel,
+        out_shape=MAP,
+        in_specs=[VMEM],
+        out_specs=VMEM,
+        compiler_params=pltpu.CompilerParams(vmem_limit_bytes=8 << 20),
+        name="settled",
+    )(x)
+
+
+def gelu_and_slope(act):
+    square = act * act
+    t = jnp.tanh(act * (GELU_C + GELU_C * GELU_A * square))
+    half = 0.5 + 0.5 * t
+    value = act * half
+    return value, half + value * (1.0 - t) * (GELU_C + 3.0 * GELU_C * GELU_A * square)
+
+
+CUTS = ((0, 384),)
 
 
 def student_kernel(first, last, *refs):
@@ -208,12 +292,16 @@
         for a, z in CUTS:
             cut = slice(a, z)
             transform(b, src[:, cut].astype(BF16), freq, cut)
+        for a, z in CUTS:
+            cut = slice(a, z)
             act[b, :, cut] = back(cut, lambda lo: times(lo, b, cut))
+        for a, z in CUTS:
+            cut = slice(a, z)
             for r in range(0, PIX, 32):
                 rows = slice(r, r + 32)
-                v = act[b, rows, cut]
-                _, cdf = gelu_parts(v)
-                gel[b, rows, cut] = (v * cdf).astype(BF16)
+                value, slope = gelu_and_slope(act[b, rows, cut])
+                gel[b, rows, cut] = value.astype(BF16)
+                act[b, rows, cut] = slope
         return jnp.dot(gel[b], point_ref[b], preferred_element_type=F32)
 
     u1[...] = x_ref[...].astype(F32) + forward(0, x_ref)
@@ -236,9 +324,7 @@
             dgel = lax.dot_general(
                 grad_low, point_ref[b, cut], (((1,), (1,)), ((), ())), preferred_element_type=F32
             )
-            v = act[b, :, cut]
-            t, _ = gelu_parts(v)
-            transform(b, (dgel * gelu_slope(v, t)).astype(BF16), dfreq, cut)
+            transform(b, (dgel * act[b, :, cut]).astype(BF16), dfreq, cut)
             if b == 1:
                 u1[:, cut] = u1[:, cut] + back(cut, lambda lo: times_conj(lo, b, cut))
             for lo in range(0, PART, 16):
@@ -362,22 +448,27 @@
     devices = 2 * CHIPS
     got = lax.ppermute(give, "dp", [(i, i ^ 1) for i in range(devices)])
     mine, *gives = fold(keep, got)
-    routes = [[(i, (i + 2 * ahead) % devices) for i in range(devices)] for ahead in (1, 2, 3)]
-    got = [lax.ppermute(block, "dp", route) for block, route in zip(gives, routes)]
+    got = []
+    for ahead in (2, 3, 1):
+        route = [(i, (i + 2 * ahead) % devices) for i in range(devices)]
+        got.append(lax.ppermute(gives[ahead - 1], "dp", route))
     point, depth = owner(mine, got)
     return jnp.swapaxes(point, 1, 2), jnp.swapaxes(depth, 1, 2)
 
 
-def from_behind(block, axis, distance):
-    devices = range(lax.axis_size(axis))
-    route = [(i - distance, i) for i in devices if i - distance in devices]
-    return lax.ppermute(block, axis, route)
+def from_behind(block, axis):
+    devices = lax.axis_size(axis)
+    return lax.ppermute(block, axis, [(i, (i + 1) % devices) for i in range(devices)])
+
+
+def from_parity(block, axis, parity):
+    devices = range(parity, lax.axis_size(axis) - 1, 2)
+    return lax.ppermute(block, axis, [(i, i + 1) for i in devices])
 
 
 def body(pipe_maps, fresh_maps, teacher_weight, student_depth, student_point):
     ticks = fresh_maps.shape[0] + 1
     weight = teacher_weight.reshape(6, 3 * CHANS, CHANS)
-    weight = pltpu.with_memory_space_constraint(weight, pltpu.HBM)
     fresh = fresh_maps.reshape(ticks - 1, PIX, CHANS)
     depth = jnp.swapaxes(student_depth, 0, 1)
     forward, inverse, taps = transforms()
@@ -387,14 +478,25 @@
     for tick in range(ticks):
         first, last = tick == 0, tick == ticks - 1
         if first:
-            teach, weight = first_teacher(current, weight)
+            teach, weight, current, point, *consts = first_teacher(
+                current, weight, student_point, *consts
+            )
+        elif last:
+            teach, current = next_teacher(
+                whole_teacher_kernel, tick - 1, moved, fresh, weight, carried[1]
+            )
         else:
-            teach, current = next_teacher(tick - 1, moved, fresh, weight, carried[1])
-        if not last:
-            moved = from_behind(teach, "section", 1)
+            odd, current = next_teacher(
+                odd_teacher_kernel, tick - 1, moved, fresh, weight, carried[1]
+            )
+            to_even = settled(from_parity(odd, "section", 1))
+            teach = even_teacher(current, weight, odd)
+            moved = (from_parity(teach, "section", 0), to_even)
+        if first:
+            moved = (from_behind(teach, "section"),)
         if last:
             extra = (jnp.asarray(taps, BF16),)
-        result = student(first, last, current, teach, consts, student_point, carried, extra)
+        result = student(first, last, current, teach, consts, point, carried, extra)
         if first:
             spectrum = result[0]
             carried, extra = tuple(result), ()

time: 67.8 us -> 64.1 us (0.945)
  the two profiles are of different devices: /device:TPU:6 before, /device:TPU:1 now
where the time goes in v1:
time: 64.1 us; the launch traced here: 63.9 us
  Pallas kernels  29.2 us (46%)
  starting transfers between devices  21.7 us (34%)
  waiting for transfers between devices  12.1 us (19%)
  between operations  0.83 us (1%)
    pallas_call x4, Pallas kernels, student(): pl.pallas_call(functools.partial(student_kernel, first, last), out_shape=...  15.5 us
    ppermute x3, starting transfers between devices, sum_at_owner(): got.append(lax.ppermute(gives[ahead - 1], 'dp', route))  8.99 us
    ppermute x3, waiting for transfers between devices, sum_at_owner(): got.append(lax.ppermute(gives[ahead - 1], 'dp', route))  7.51 us
    ppermute x4, starting transfers between devices, from_parity(): return lax.ppermute(block, axis, [(i, i + 1) for i in devices])  6.04 us
    pallas_call x2, Pallas kernels, even_teacher(): pl.pallas_call(even_teacher_kernel, out_shape=MAP, in_specs=[VMEM] * 3, o...  5.23 us
    pallas_call x1, Pallas kernels, first_teacher(): pl.pallas_call(first_teacher_kernel, out_shape=[MAP, *held], in_specs=[pl...  4.71 us
    ppermute x1, starting transfers between devices, sum_at_owner(): got = lax.ppermute(give, 'dp', [(i, i ^ 1) for i in range(devices)])  4.16 us
    ppermute x1, waiting for transfers between devices, from_behind(): lax.ppermute(block, axis, [(i, (i + 1) % devices) for i in range(devices)])  3.31 us
  transfers between devices with their start and end apart: 9, of which 4 were waited for; matrix products, arithmetic and copies ran while one was open for 0% of the time, Pallas kernels for 26%

profile of v1, /device:TPU:1, one launch (start us, length us, event | category | flops | bytes accessed | tf_op | source)
XLA Modules:
  0.0 63.9 jit_solution(1115703876312806080)
XLA Ops:
  0.6 0.0 copy-start.2
  0.6 0.0 copy-start.3
  0.7 4.7 %teacher.4 = (bf16[256,384]{1,0:T(8,128)(2,1)S(1)}, bf16[6,1152,384]{2,1,0:T(8,128)(2,1)S(1)}, bf16[256,384]{1,0:T(8,128)(2,1)S(1)}, bf16[2,384,384]{2,1,0:T(8,1...) custom-call(bf16[256,384]{1,0:T(8,128)(2,1)} %bitcast.12, bf16[6,1152,384]{2,1,0:T(8,128)(2,1)} %bitcast.11, ...), custom_call_target="tpu_custom_call" | custom-call | flops 1358954496 | bytes 5308416 | tf_op jit(solution)/shard_map/teacher/pallas_call | solution.py:164
  5.4 2.6 %collective-permute-start = (bf16[256,384]{1,0:T(8,128)(2,1)S(1)}, bf16[256,384]{1,0:T(8,128)(2,1)S(1)}, u32[]{:S(2)}, u32[]{:S(2)}) collective-permute-start(bf16[256,384]{1,0:T(8,128)(2,1)S(1)} %get-tuple-element.33.refs_1_), channel_id=1, source_target_pairs={{0,8},{8,16},{16,24},{24,32},{32,40},{40,48},{48,56},{56,64},{64,7... | collective-permute-start | bytes 589832 | tf_op jit(solution)/shard_map/ppermute | solution.py:461
  7.9 0.0 copy-done.2
  7.9 0.0 copy-done.3
  7.9 0.0 copy-start
  7.9 4.4 %student.4 = (f32[2,416,384]{2,1,0:T(8,128)S(1)}, f32[2,384,384]{2,1,0:T(8,128)S(1)}, f32[2,416,384]{2,1,0:T(8,128)S(1)}) custom-call(bf16[256,384]{1,0:T(8,128)(2,1)S(1)} %get-tuple-element.32.refs_0_, bf16[256,384]{1,0:T(8,128)(2,1)S(1)} %get-tuple-element.33.refs_1_, bf16[416,256]{1,0:T(8,128)(2,1)S(1)} %get-tuple-element.34.refs_2_, ...), custom_call_target="tpu_custom_call" | custom-call | flops 981467136 | bytes 8388608 | tf_op jit(solution)/shard_map/student/pallas_call | solution.py:373
  12.3 3.3 %collective-permute-done.refs_0_ = bf16[256,384]{1,0:T(8,128)(2,1)S(1)} collective-permute-done((bf16[256,384]{1,0:T(8,128)(2,1)S(1)}, bf16[256,384]{1,0:T(8,128)(2,1)S(1)}, u32[]{:S(2)}, u32[]{:S(2)}) %collective-permute-start) | collective-permute-done | bytes 196640 | tf_op jit(solution)/shard_map/ppermute | solution.py:461
  15.6 0.0 copy-done
  15.7 0.7 %collective-permute-start.2 = (bf16[256,384]{1,0:T(8,128)(2,1)S(1)}, bf16[256,384]{1,0:T(8,128)(2,1)S(1)}, u32[]{:S(2)}, u32[]{:S(2)}) collective-permute-start(bf16[256,384]{1,0:T(8,128)(2,1)S(1)} %get-tuple-element.39.odd_ref), channel_id=1, source_target_pairs={{8,16},{24,32},{40,48},{56,64},{72,80},{88,96},{104,112},{120,128}... | collective-permute-start | bytes 589832 | tf_op jit(solution)/shard_map/ppermute | solution.py:466
  16.4 2.6 %teacher_even.2.refs_1_ = bf16[256,384]{1,0:T(8,128)(2,1)S(1)} custom-call(bf16[256,384]{1,0:T(8,128)(2,1)S(1)} %get-tuple-element.38.x_ref.refs_0_, bf16[6,1152,384]{2,1,0:T(8,128)(2,1)S(1)} %get-tuple-element.31.w_ref, bf16[256,384]{1,0:T(8,128)(2,1)S(1)} %get-tuple-element.39.odd_ref), custom_call_target="tpu_custom_call" | custom-call | flops 1358954496 | bytes 5308416 | tf_op jit(solution)/shard_map/teacher_even/pallas_call | solution.py:194
  19.0 1.5 %collective-permute-start.1 = (bf16[256,384]{1,0:T(8,128)(2,1)S(1)}, bf16[256,384]{1,0:T(8,128)(2,1)S(1)}, u32[]{:S(2)}, u32[]{:S(2)}) collective-permute-start(bf16[256,384]{1,0:T(8,128)(2,1)S(1)} %teacher_even.2.refs_1_), channel_id=1, source_target_pairs={{0,8},{16,24},{32,40},{48,56},{64,72},{80,88},{96,104},{112,120},{... | collective-permute-start | bytes 589832 | tf_op jit(solution)/shard_map/ppermute | solution.py:466
  20.5 3.6 %student.5 = (f32[2,384,384]{2,1,0:T(8,128)S(1)}, f32[2,416,384]{2,1,0:T(8,128)S(1)}) custom-call(bf16[256,384]{1,0:T(8,128)(2,1)S(1)} %get-tuple-element.38.x_ref.refs_0_, bf16[256,384]{1,0:T(8,128)(2,1)S(1)} %teacher_even.2.refs_1_, bf16[416,256]{1,0:T(8,128)(2,1)S(1)} %get-tuple-element.34.refs_2_, ...), custom_call_target="tpu_custom_call", output_to_operand_aliasing={{0}: (6, {}), {1}: (7, {})} | custom-call | flops 981467136 | bytes 8388608 | tf_op jit(solution)/shard_map/student/pallas_call | solution.py:373
  24.1 0.0 collective-permute-done.2.x_ref
  24.1 0.0 collective-permute-done.1.refs_0_
  24.1 0.1 teacher.6
  24.2 0.7 %collective-permute-start.4 = (bf16[256,384]{1,0:T(8,128)(2,1)S(1)}, bf16[256,384]{1,0:T(8,128)(2,1)S(1)}, u32[]{:S(2)}, u32[]{:S(2)}) collective-permute-start(bf16[256,384]{1,0:T(8,128)(2,1)S(1)} %get-tuple-element.44.odd_ref), channel_id=1, source_target_pairs={{8,16},{24,32},{40,48},{56,64},{72,80},{88,96},{104,112},{120,128}... | collective-permute-start | bytes 589832 | tf_op jit(solution)/shard_map/ppermute | solution.py:466
  24.9 2.6 %teacher_even.3.refs_1_ = bf16[256,384]{1,0:T(8,128)(2,1)S(1)} custom-call(bf16[256,384]{1,0:T(8,128)(2,1)S(1)} %get-tuple-element.43.x_ref.refs_0_, bf16[6,1152,384]{2,1,0:T(8,128)(2,1)S(1)} %get-tuple-element.31.w_ref, bf16[256,384]{1,0:T(8,128)(2,1)S(1)} %get-tuple-element.44.odd_ref), custom_call_target="tpu_custom_call" | custom-call | flops 1358954496 | bytes 5308416 | tf_op jit(solution)/shard_map/teacher_even/pallas_call | solution.py:194
  27.5 3.2 %collective-permute-start.3 = (bf16[256,384]{1,0:T(8,128)(2,1)S(1)}, bf16[256,384]{1,0:T(8,128)(2,1)S(1)}, u32[]{:S(2)}, u32[]{:S(2)}) collective-permute-start(bf16[256,384]{1,0:T(8,128)(2,1)S(1)} %teacher_even.3.refs_1_), channel_id=1, source_target_pairs={{0,8},{16,24},{32,40},{48,56},{64,72},{80,88},{96,104},{112,120},{... | collective-permute-start | bytes 589832 | tf_op jit(solution)/shard_map/ppermute | solution.py:466
  30.7 3.6 %student.6 = (f32[2,384,384]{2,1,0:T(8,128)S(1)}, f32[2,416,384]{2,1,0:T(8,128)S(1)}) custom-call(bf16[256,384]{1,0:T(8,128)(2,1)S(1)} %get-tuple-element.43.x_ref.refs_0_, bf16[256,384]{1,0:T(8,128)(2,1)S(1)} %teacher_even.3.refs_1_, bf16[416,256]{1,0:T(8,128)(2,1)S(1)} %get-tuple-element.34.refs_2_, ...), custom_call_target="tpu_custom_call", output_to_operand_aliasing={{0}: (6, {}), {1}: (7, {})} | custom-call | flops 981467136 | bytes 8388608 | tf_op jit(solution)/shard_map/student/pallas_call | solution.py:373
  34.3 0.0 collective-permute-done.4.x_ref
  34.3 0.0 collective-permute-done.3.refs_0_
  34.3 0.0 copy-start.1
  34.3 2.9 %teacher.7 = (bf16[256,384]{1,0:T(8,128)(2,1)S(1)}, bf16[256,384]{1,0:T(8,128)(2,1)S(1)}) custom-call(bf16[3,256,384]{2,1,0:T(8,128)(2,1)S(1)} %bitcast.9, bf16[6,1152,384]{2,1,0:T(8,128)(2,1)S(1)} %get-tuple-element.31.w_ref, f32[2,384,384]{2,1,0:T(8,128)S(1)} %get-tuple-element.46.after.refs_6_, bf16[256,384]{1,0:T(8,128)(2,1)S(1)} %collective-permute-done.3.refs_0_, ...), custom_call_target="tpu_custom_call" | custom-call | flops 1358954496 | bytes 5308416 | tf_op jit(solution)/shard_map/teacher/pallas_call | solution.py:181
  37.2 0.0 copy-done.1
  37.2 4.0 %student.7 = (bf16[4,48,896]{2,1,0:T(8,128)(2,1)S(1)}, bf16[4,48,896]{2,1,0:T(8,128)(2,1)S(1)}, bf16[256,384]{1,0:T(8,128)(2,1)}) custom-call(bf16[256,384]{1,0:T(8,128)(2,1)S(1)} %get-tuple-element.47.refs_0_, bf16[256,384]{1,0:T(8,128)(2,1)S(1)} %get-tuple-element.48.refs_1_, bf16[416,256]{1,0:T(8,128)(2,1)S(1)} %get-tuple-element.34.refs_2_, ...), custom_call_target="tpu_custom_call" | custom-call | flops 981467136 | bytes 8388608 | tf_op jit(solution)/shard_map/student/pallas_call | solution.py:373
  41.2 4.2 %collective-permute-start.5 = (bf16[4,48,896]{2,1,0:T(8,128)(2,1)S(1)}, bf16[4,48,896]{2,1,0:T(8,128)(2,1)S(1)}, u32[]{:S(2)}, u32[]{:S(2)}) collective-permute-start(bf16[4,48,896]{2,1,0:T(8,128)(2,1)S(1)} %get-tuple-element.52), channel_id=1, source_target_pairs={{0,1},{1,0},{2,3},{3,2},{4,5},{5,4},{6,7},{7,6},{8,9},{9,8},{10,11... | collective-permute-start | bytes 1032200 | tf_op jit(solution)/shard_map/ppermute | solution.py:449
  45.3 1.3 %collective-permute-done.5.got_ref = bf16[4,48,896]{2,1,0:T(8,128)(2,1)S(1)} collective-permute-done((bf16[4,48,896]{2,1,0:T(8,128)(2,1)S(1)}, bf16[4,48,896]{2,1,0:T(8,128)(2,1)S(1)}, u32[]{:S(2)}, u32[]{:S(2)}) %collective-permute-start.5) | collective-permute-done | bytes 344096 | tf_op jit(solution)/shard_map/ppermute | solution.py:449
  46.6 0.1 fold_cores.1
  46.7 6.6 %collective-permute-start.6 = (bf16[48,896]{1,0:T(8,128)(2,1)S(1)}, bf16[48,896]{1,0:T(8,128)(2,1)S(1)}, u32[]{:S(2)}, u32[]{:S(2)}) collective-permute-start(bf16[48,896]{1,0:T(8,128)(2,1)S(1)} %get-tuple-element.54), channel_id=1, source_target_pairs={{0,4},{1,5},{2,6},{3,7},{4,0},{5,1},{6,2},{7,3},{8,12},{9,13},{10,... | collective-permute-start | bytes 258056 | tf_op jit(solution)/shard_map/ppermute | solution.py:454
  53.3 0.3 collective-permute-start.7
  53.6 2.1 %collective-permute-start.8 = (bf16[48,896]{1,0:T(8,128)(2,1)S(1)}, bf16[48,896]{1,0:T(8,128)(2,1)S(1)}, u32[]{:S(2)}, u32[]{:S(2)}) collective-permute-start(bf16[48,896]{1,0:T(8,128)(2,1)S(1)} %get-tuple-element.56), channel_id=1, source_target_pairs={{0,2},{1,3},{2,4},{3,5},{4,6},{5,7},{6,0},{7,1},{8,10},{9,11},{10,... | collective-permute-start | bytes 258056 | tf_op jit(solution)/shard_map/ppermute | solution.py:454
  55.7 0.2 collective-permute-done.6.refs_0_
  55.9 7.3 %collective-permute-done.7.refs_1_ = bf16[48,896]{1,0:T(8,128)(2,1)S(1)} collective-permute-done((bf16[48,896]{1,0:T(8,128)(2,1)S(1)}, bf16[48,896]{1,0:T(8,128)(2,1)S(1)}, u32[]{:S(2)}, u32[]{:S(2)}) %collective-permute-start.7) | collective-permute-done | bytes 86048 | tf_op jit(solution)/shard_map/ppermute | solution.py:454
  63.2 0.0 collective-permute-done.8.refs_2_
  63.2 0.7 %owner_sum.1 = (f32[2,48,384]{2,1,0:T(8,128)}, f32[2,48,49]{2,1,0:T(8,128)}) custom-call(f32[48,896]{1,0:T(8,128)S(1)} %get-tuple-element.53.mine_ref, bf16[48,896]{1,0:T(8,128)(2,1)S(1)} %collective-permute-done.6.refs_0_, bf16[48,896]{1,0:T(8,128)(2,1)S(1)} %collective-permute-done.7.refs_1_, bf16[48,896]{1,0:T(8,128)(2,1)S(1)} %collective-permute-done.8.refs_2_), custom_call_target="tpu_custom_call" | custom-call | tf_op jit(solution)/shard_map/owner_sum/pallas_call | solution.py:434
  (3 shorter events, 0.1 us)
Async XLA Ops:
  0.6 7.3 %copy-start.2 = (f32[2,49,384]{2,0,1:T(2,128)S(1)}, f32[2,49,384]{2,0,1:T(2,128)}, u32[]{:S(2)}) copy-start(f32[2,49,384]{2,0,1:T(2,128)} %param.12) | copy-start | bytes 451588
  0.6 7.3 %copy-start.3 = (f32[416,64]{1,0:T(8,128)S(1)}, f32[416,64]{1,0:T(8,128)}, u32[]{:S(2)}) copy-start(f32[416,64]{1,0:T(8,128)} %constant.10.clone.refs_5_) | copy-start | bytes 319492
  5.4 10.3 %collective-permute-start = (bf16[256,384]{1,0:T(8,128)(2,1)S(1)}, bf16[256,384]{1,0:T(8,128)(2,1)S(1)}, u32[]{:S(2)}, u32[]{:S(2)}) collective-permute-start(bf16[256,384]{1,0:T(8,128)(2,1)S(1)} %get-tuple-element.33.refs_1_), channel_id=1, source_target_pairs={{0,8},{8,16},{16,24},{24,32},{32,40},{40,48},{48,56},{56,64},{64,7... | collective-permute-start | bytes 589832 | tf_op jit(solution)/shard_map/ppermute | solution.py:461
  7.9 7.7 %copy-start = (bf16[3,1,8,32,384]{4,3,2,1,0:T(8,128)(2,1)S(1)}, bf16[3,1,8,32,384]{4,3,2,1,0:T(8,128)(2,1)}, u32[]{:S(2)}) copy-start(bf16[3,1,8,32,384]{4,3,2,1,0:T(8,128)(2,1)} %param.10) | copy-start | bytes 1769476
  15.7 8.4 %collective-permute-start.2 = (bf16[256,384]{1,0:T(8,128)(2,1)S(1)}, bf16[256,384]{1,0:T(8,128)(2,1)S(1)}, u32[]{:S(2)}, u32[]{:S(2)}) collective-permute-start(bf16[256,384]{1,0:T(8,128)(2,1)S(1)} %get-tuple-element.39.odd_ref), channel_id=1, source_target_pairs={{8,16},{24,32},{40,48},{56,64},{72,80},{88,96},{104,112},{120,128}... | collective-permute-start | bytes 589832 | tf_op jit(solution)/shard_map/ppermute | solution.py:466
  19.0 5.1 %collective-permute-start.1 = (bf16[256,384]{1,0:T(8,128)(2,1)S(1)}, bf16[256,384]{1,0:T(8,128)(2,1)S(1)}, u32[]{:S(2)}, u32[]{:S(2)}) collective-permute-start(bf16[256,384]{1,0:T(8,128)(2,1)S(1)} %teacher_even.2.refs_1_), channel_id=1, source_target_pairs={{0,8},{16,24},{32,40},{48,56},{64,72},{80,88},{96,104},{112,120},{... | collective-permute-start | bytes 589832 | tf_op jit(solution)/shard_map/ppermute | solution.py:466
  24.2 10.1 %collective-permute-start.4 = (bf16[256,384]{1,0:T(8,128)(2,1)S(1)}, bf16[256,384]{1,0:T(8,128)(2,1)S(1)}, u32[]{:S(2)}, u32[]{:S(2)}) collective-permute-start(bf16[256,384]{1,0:T(8,128)(2,1)S(1)} %get-tuple-element.44.odd_ref), channel_id=1, source_target_pairs={{8,16},{24,32},{40,48},{56,64},{72,80},{88,96},{104,112},{120,128}... | collective-permute-start | bytes 589832 | tf_op jit(solution)/shard_map/ppermute | solution.py:466
  27.5 6.8 %collective-permute-start.3 = (bf16[256,384]{1,0:T(8,128)(2,1)S(1)}, bf16[256,384]{1,0:T(8,128)(2,1)S(1)}, u32[]{:S(2)}, u32[]{:S(2)}) collective-permute-start(bf16[256,384]{1,0:T(8,128)(2,1)S(1)} %teacher_even.3.refs_1_), channel_id=1, source_target_pairs={{0,8},{16,24},{32,40},{48,56},{64,72},{80,88},{96,104},{112,120},{... | collective-permute-start | bytes 589832 | tf_op jit(solution)/shard_map/ppermute | solution.py:466
  34.3 2.9 %copy-start.1 = (bf16[416,64]{1,0:T(8,128)(2,1)S(1)}, bf16[416,64]{1,0:T(8,128)(2,1)}, u32[]{:S(2)}) copy-start(bf16[416,64]{1,0:T(8,128)(2,1)} %constant.11.clone.refs_8_) | copy-start | bytes 159748
  41.2 5.4 %collective-permute-start.5 = (bf16[4,48,896]{2,1,0:T(8,128)(2,1)S(1)}, bf16[4,48,896]{2,1,0:T(8,128)(2,1)S(1)}, u32[]{:S(2)}, u32[]{:S(2)}) collective-permute-start(bf16[4,48,896]{2,1,0:T(8,128)(2,1)S(1)} %get-tuple-element.52), channel_id=1, source_target_pairs={{0,1},{1,0},{2,3},{3,2},{4,5},{5,4},{6,7},{7,6},{8,9},{9,8},{10,11... | collective-permute-start | bytes 1032200 | tf_op jit(solution)/shard_map/ppermute | solution.py:449
  46.7 9.2 %collective-permute-start.6 = (bf16[48,896]{1,0:T(8,128)(2,1)S(1)}, bf16[48,896]{1,0:T(8,128)(2,1)S(1)}, u32[]{:S(2)}, u32[]{:S(2)}) collective-permute-start(bf16[48,896]{1,0:T(8,128)(2,1)S(1)} %get-tuple-element.54), channel_id=1, source_target_pairs={{0,4},{1,5},{2,6},{3,7},{4,0},{5,1},{6,2},{7,3},{8,12},{9,13},{10,... | collective-permute-start | bytes 258056 | tf_op jit(solution)/shard_map/ppermute | solution.py:454
  53.3 9.9 %collective-permute-start.7 = (bf16[48,896]{1,0:T(8,128)(2,1)S(1)}, bf16[48,896]{1,0:T(8,128)(2,1)S(1)}, u32[]{:S(2)}, u32[]{:S(2)}) collective-permute-start(bf16[48,896]{1,0:T(8,128)(2,1)S(1)} %get-tuple-element.55), channel_id=1, source_target_pairs={{0,6},{1,7},{2,0},{3,1},{4,2},{5,3},{6,4},{7,5},{8,14},{9,15},{10,... | collective-permute-start | bytes 258056 | tf_op jit(solution)/shard_map/ppermute | solution.py:454
  53.6 9.6 %collective-permute-start.8 = (bf16[48,896]{1,0:T(8,128)(2,1)S(1)}, bf16[48,896]{1,0:T(8,128)(2,1)S(1)}, u32[]{:S(2)}, u32[]{:S(2)}) collective-permute-start(bf16[48,896]{1,0:T(8,128)(2,1)S(1)} %get-tuple-element.56), channel_id=1, source_target_pairs={{0,2},{1,3},{2,4},{3,5},{4,6},{5,7},{6,0},{7,1},{8,10},{9,11},{10,... | collective-permute-start | bytes 258056 | tf_op jit(solution)/shard_map/ppermute | solution.py:454

commit v2 on v1

--- a/solution.py
+++ b/solution.py
@@ -403,7 +403,7 @@
 
     mine_ref[...] = block(chip)
     for ahead, ref in enumerate(give_refs, 1):
-        ref[...] = block((chip + ahead) % CHIPS).astype(BF16)
+        ref[...] = block(chip ^ ahead).astype(BF16)
 
 
 def fold(keep, got):
@@ -449,8 +449,8 @@
     got = lax.ppermute(give, "dp", [(i, i ^ 1) for i in range(devices)])
     mine, *gives = fold(keep, got)
     got = []
-    for ahead in (2, 3, 1):
-        route = [(i, (i + 2 * ahead) % devices) for i in range(devices)]
+    for ahead in (1, 2, 3):
+        route = [(i, i ^ (2 * ahead)) for i in range(devices)]
         got.append(lax.ppermute(gives[ahead - 1], "dp", route))
     point, depth = owner(mine, got)
     return jnp.swapaxes(point, 1, 2), jnp.swapaxes(depth, 1, 2)

time: 64.1 us -> 63.3 us (0.988)
  the two profiles are of different devices: /device:TPU:1 before, /device:TPU:6 now
where the time goes in v2:
time: 63.3 us; the launch traced here: 62.7 us
  Pallas kernels  29.2 us (46%)
  starting transfers between devices  17.3 us (27%)
  waiting for transfers between devices  15.4 us (24%)
  between operations  0.82 us (1%)
    pallas_call x4, Pallas kernels, student(): pl.pallas_call(functools.partial(student_kernel, first, last), out_shape=...  15.5 us
    ppermute x3, starting transfers between devices, sum_at_owner(): got.append(lax.ppermute(gives[ahead - 1], 'dp', route))  8.76 us
    ppermute x3, waiting for transfers between devices, sum_at_owner(): got.append(lax.ppermute(gives[ahead - 1], 'dp', route))  7.34 us
    ppermute x4, starting transfers between devices, from_parity(): return lax.ppermute(block, axis, [(i, i + 1) for i in devices])  6.53 us
    pallas_call x2, Pallas kernels, even_teacher(): pl.pallas_call(even_teacher_kernel, out_shape=MAP, in_specs=[VMEM] * 3, o...  5.24 us
    pallas_call x1, Pallas kernels, first_teacher(): pl.pallas_call(first_teacher_kernel, out_shape=[MAP, *held], in_specs=[pl...  4.73 us
    ppermute x1, waiting for transfers between devices, from_behind(): lax.ppermute(block, axis, [(i, (i + 1) % devices) for i in range(devices)])  3.34 us
    ppermute x4, waiting for transfers between devices, from_parity(): return lax.ppermute(block, axis, [(i, i + 1) for i in devices])  3.04 us
  transfers between devices with their start and end apart: 9, of which 6 were waited for; matrix products, arithmetic and copies ran while one was open for 0% of the time, Pallas kernels for 27%

profile of v2, /device:TPU:6, one launch (start us, length us, event | category | flops | bytes accessed | tf_op | source)
XLA Modules:
  0.0 62.7 jit_solution(16570136004661101364)
XLA Ops:
  0.6 0.0 copy-start.2
  0.6 0.0 copy-start.3
  0.7 4.7 %teacher.4 = (bf16[256,384]{1,0:T(8,128)(2,1)S(1)}, bf16[6,1152,384]{2,1,0:T(8,128)(2,1)S(1)}, bf16[256,384]{1,0:T(8,128)(2,1)S(1)}, bf16[2,384,384]{2,1,0:T(8,1...) custom-call(bf16[256,384]{1,0:T(8,128)(2,1)} %bitcast.12, bf16[6,1152,384]{2,1,0:T(8,128)(2,1)} %bitcast.11, ...), custom_call_target="tpu_custom_call" | custom-call | flops 1358954496 | bytes 5308416 | tf_op jit(solution)/shard_map/teacher/pallas_call | solution.py:164
  5.4 2.0 %collective-permute-start = (bf16[256,384]{1,0:T(8,128)(2,1)S(1)}, bf16[256,384]{1,0:T(8,128)(2,1)S(1)}, u32[]{:S(2)}, u32[]{:S(2)}) collective-permute-start(bf16[256,384]{1,0:T(8,128)(2,1)S(1)} %get-tuple-element.33.refs_1_), channel_id=1, source_target_pairs={{0,8},{8,16},{16,24},{24,32},{32,40},{40,48},{48,56},{56,64},{64,7... | collective-permute-start | bytes 589832 | tf_op jit(solution)/shard_map/ppermute | solution.py:461
  7.4 0.0 copy-done.2
  7.4 0.0 copy-done.3
  7.4 0.0 copy-start
  7.4 4.4 %student.4 = (f32[2,416,384]{2,1,0:T(8,128)S(1)}, f32[2,384,384]{2,1,0:T(8,128)S(1)}, f32[2,416,384]{2,1,0:T(8,128)S(1)}) custom-call(bf16[256,384]{1,0:T(8,128)(2,1)S(1)} %get-tuple-element.32.refs_0_, bf16[256,384]{1,0:T(8,128)(2,1)S(1)} %get-tuple-element.33.refs_1_, bf16[416,256]{1,0:T(8,128)(2,1)S(1)} %get-tuple-element.34.refs_2_, ...), custom_call_target="tpu_custom_call" | custom-call | flops 981467136 | bytes 8388608 | tf_op jit(solution)/shard_map/student/pallas_call | solution.py:373
  11.8 3.3 %collective-permute-done.refs_0_ = bf16[256,384]{1,0:T(8,128)(2,1)S(1)} collective-permute-done((bf16[256,384]{1,0:T(8,128)(2,1)S(1)}, bf16[256,384]{1,0:T(8,128)(2,1)S(1)}, u32[]{:S(2)}, u32[]{:S(2)}) %collective-permute-start) | collective-permute-done | bytes 196640 | tf_op jit(solution)/shard_map/ppermute | solution.py:461
  15.1 0.0 copy-done
  15.1 1.3 %collective-permute-start.2 = (bf16[256,384]{1,0:T(8,128)(2,1)S(1)}, bf16[256,384]{1,0:T(8,128)(2,1)S(1)}, u32[]{:S(2)}, u32[]{:S(2)}) collective-permute-start(bf16[256,384]{1,0:T(8,128)(2,1)S(1)} %get-tuple-element.39.odd_ref), channel_id=1, source_target_pairs={{8,16},{24,32},{40,48},{56,64},{72,80},{88,96},{104,112},{120,128}... | collective-permute-start | bytes 589832 | tf_op jit(solution)/shard_map/ppermute | solution.py:466
  16.4 2.6 %teacher_even.2.refs_1_ = bf16[256,384]{1,0:T(8,128)(2,1)S(1)} custom-call(bf16[256,384]{1,0:T(8,128)(2,1)S(1)} %get-tuple-element.38.x_ref.refs_0_, bf16[6,1152,384]{2,1,0:T(8,128)(2,1)S(1)} %get-tuple-element.31.w_ref, bf16[256,384]{1,0:T(8,128)(2,1)S(1)} %get-tuple-element.39.odd_ref), custom_call_target="tpu_custom_call" | custom-call | flops 1358954496 | bytes 5308416 | tf_op jit(solution)/shard_map/teacher_even/pallas_call | solution.py:194
  19.1 1.5 %collective-permute-start.1 = (bf16[256,384]{1,0:T(8,128)(2,1)S(1)}, bf16[256,384]{1,0:T(8,128)(2,1)S(1)}, u32[]{:S(2)}, u32[]{:S(2)}) collective-permute-start(bf16[256,384]{1,0:T(8,128)(2,1)S(1)} %teacher_even.2.refs_1_), channel_id=1, source_target_pairs={{0,8},{16,24},{32,40},{48,56},{64,72},{80,88},{96,104},{112,120},{... | collective-permute-start | bytes 589832 | tf_op jit(solution)/shard_map/ppermute | solution.py:466
  20.5 3.6 %student.5 = (f32[2,384,384]{2,1,0:T(8,128)S(1)}, f32[2,416,384]{2,1,0:T(8,128)S(1)}) custom-call(bf16[256,384]{1,0:T(8,128)(2,1)S(1)} %get-tuple-element.38.x_ref.refs_0_, bf16[256,384]{1,0:T(8,128)(2,1)S(1)} %teacher_even.2.refs_1_, bf16[416,256]{1,0:T(8,128)(2,1)S(1)} %get-tuple-element.34.refs_2_, ...), custom_call_target="tpu_custom_call", output_to_operand_aliasing={{0}: (6, {}), {1}: (7, {})} | custom-call | flops 981467136 | bytes 8388608 | tf_op jit(solution)/shard_map/student/pallas_call | solution.py:373
  24.1 1.6 %collective-permute-done.2.x_ref = bf16[256,384]{1,0:T(8,128)(2,1)S(1)} collective-permute-done((bf16[256,384]{1,0:T(8,128)(2,1)S(1)}, bf16[256,384]{1,0:T(8,128)(2,1)S(1)}, u32[]{:S(2)}, u32[]{:S(2)}) %collective-permute-start.2) | collective-permute-done | bytes 196640 | tf_op jit(solution)/shard_map/ppermute | solution.py:466
  25.8 0.0 collective-permute-done.1.refs_0_
  25.8 0.1 teacher.6
  25.9 1.3 %collective-permute-start.4 = (bf16[256,384]{1,0:T(8,128)(2,1)S(1)}, bf16[256,384]{1,0:T(8,128)(2,1)S(1)}, u32[]{:S(2)}, u32[]{:S(2)}) collective-permute-start(bf16[256,384]{1,0:T(8,128)(2,1)S(1)} %get-tuple-element.44.odd_ref), channel_id=1, source_target_pairs={{8,16},{24,32},{40,48},{56,64},{72,80},{88,96},{104,112},{120,128}... | collective-permute-start | bytes 589832 | tf_op jit(solution)/shard_map/ppermute | solution.py:466
  27.2 2.6 %teacher_even.3.refs_1_ = bf16[256,384]{1,0:T(8,128)(2,1)S(1)} custom-call(bf16[256,384]{1,0:T(8,128)(2,1)S(1)} %get-tuple-element.43.x_ref.refs_0_, bf16[6,1152,384]{2,1,0:T(8,128)(2,1)S(1)} %get-tuple-element.31.w_ref, bf16[256,384]{1,0:T(8,128)(2,1)S(1)} %get-tuple-element.44.odd_ref), custom_call_target="tpu_custom_call" | custom-call | flops 1358954496 | bytes 5308416 | tf_op jit(solution)/shard_map/teacher_even/pallas_call | solution.py:194
  29.8 2.5 %collective-permute-start.3 = (bf16[256,384]{1,0:T(8,128)(2,1)S(1)}, bf16[256,384]{1,0:T(8,128)(2,1)S(1)}, u32[]{:S(2)}, u32[]{:S(2)}) collective-permute-start(bf16[256,384]{1,0:T(8,128)(2,1)S(1)} %teacher_even.3.refs_1_), channel_id=1, source_target_pairs={{0,8},{16,24},{32,40},{48,56},{64,72},{80,88},{96,104},{112,120},{... | collective-permute-start | bytes 589832 | tf_op jit(solution)/shard_map/ppermute | solution.py:466
  32.3 3.6 %student.6 = (f32[2,384,384]{2,1,0:T(8,128)S(1)}, f32[2,416,384]{2,1,0:T(8,128)S(1)}) custom-call(bf16[256,384]{1,0:T(8,128)(2,1)S(1)} %get-tuple-element.43.x_ref.refs_0_, bf16[256,384]{1,0:T(8,128)(2,1)S(1)} %teacher_even.3.refs_1_, bf16[416,256]{1,0:T(8,128)(2,1)S(1)} %get-tuple-element.34.refs_2_, ...), custom_call_target="tpu_custom_call", output_to_operand_aliasing={{0}: (6, {}), {1}: (7, {})} | custom-call | flops 981467136 | bytes 8388608 | tf_op jit(solution)/shard_map/student/pallas_call | solution.py:373
  35.8 1.4 %collective-permute-done.4.x_ref = bf16[256,384]{1,0:T(8,128)(2,1)S(1)} collective-permute-done((bf16[256,384]{1,0:T(8,128)(2,1)S(1)}, bf16[256,384]{1,0:T(8,128)(2,1)S(1)}, u32[]{:S(2)}, u32[]{:S(2)}) %collective-permute-start.4) | collective-permute-done | bytes 196640 | tf_op jit(solution)/shard_map/ppermute | solution.py:466
  37.3 0.0 collective-permute-done.3.refs_0_
  37.3 0.0 copy-start.1
  37.3 2.9 %teacher.7 = (bf16[256,384]{1,0:T(8,128)(2,1)S(1)}, bf16[256,384]{1,0:T(8,128)(2,1)S(1)}) custom-call(bf16[3,256,384]{2,1,0:T(8,128)(2,1)S(1)} %bitcast.9, bf16[6,1152,384]{2,1,0:T(8,128)(2,1)S(1)} %get-tuple-element.31.w_ref, f32[2,384,384]{2,1,0:T(8,128)S(1)} %get-tuple-element.46.after.refs_6_, bf16[256,384]{1,0:T(8,128)(2,1)S(1)} %collective-permute-done.3.refs_0_, ...), custom_call_target="tpu_custom_call" | custom-call | flops 1358954496 | bytes 5308416 | tf_op jit(solution)/shard_map/teacher/pallas_call | solution.py:181
  40.2 0.0 copy-done.1
  40.2 3.9 %student.7 = (bf16[4,48,896]{2,1,0:T(8,128)(2,1)S(1)}, bf16[4,48,896]{2,1,0:T(8,128)(2,1)S(1)}, bf16[256,384]{1,0:T(8,128)(2,1)}) custom-call(bf16[256,384]{1,0:T(8,128)(2,1)S(1)} %get-tuple-element.47.refs_0_, bf16[256,384]{1,0:T(8,128)(2,1)S(1)} %get-tuple-element.48.refs_1_, bf16[416,256]{1,0:T(8,128)(2,1)S(1)} %get-tuple-element.34.refs_2_, ...), custom_call_target="tpu_custom_call" | custom-call | flops 981467136 | bytes 8388608 | tf_op jit(solution)/shard_map/student/pallas_call | solution.py:373
  44.1 0.1 collective-permute-start.5
  44.2 1.6 %collective-permute-done.5.got_ref = bf16[4,48,896]{2,1,0:T(8,128)(2,1)S(1)} collective-permute-done((bf16[4,48,896]{2,1,0:T(8,128)(2,1)S(1)}, bf16[4,48,896]{2,1,0:T(8,128)(2,1)S(1)}, u32[]{:S(2)}, u32[]{:S(2)}) %collective-permute-start.5) | collective-permute-done | bytes 344096 | tf_op jit(solution)/shard_map/ppermute | solution.py:449
  45.8 0.1 fold_cores.1
  45.9 3.4 %collective-permute-start.6 = (bf16[48,896]{1,0:T(8,128)(2,1)S(1)}, bf16[48,896]{1,0:T(8,128)(2,1)S(1)}, u32[]{:S(2)}, u32[]{:S(2)}) collective-permute-start(bf16[48,896]{1,0:T(8,128)(2,1)S(1)} %get-tuple-element.54), channel_id=1, source_target_pairs={{0,2},{1,3},{2,0},{3,1},{4,6},{5,7},{6,4},{7,5},{8,10},{9,11},{10,... | collective-permute-start | bytes 258056 | tf_op jit(solution)/shard_map/ppermute | solution.py:454
  49.3 5.4 %collective-permute-start.7 = (bf16[48,896]{1,0:T(8,128)(2,1)S(1)}, bf16[48,896]{1,0:T(8,128)(2,1)S(1)}, u32[]{:S(2)}, u32[]{:S(2)}) collective-permute-start(bf16[48,896]{1,0:T(8,128)(2,1)S(1)} %get-tuple-element.55), channel_id=1, source_target_pairs={{0,4},{1,5},{2,6},{3,7},{4,0},{5,1},{6,2},{7,3},{8,12},{9,13},{10,... | collective-permute-start | bytes 258056 | tf_op jit(solution)/shard_map/ppermute | solution.py:454
  54.7 0.0 collective-permute-start.8
  54.7 0.0 collective-permute-done.6.refs_0_
  54.7 6.4 %collective-permute-done.7.refs_1_ = bf16[48,896]{1,0:T(8,128)(2,1)S(1)} collective-permute-done((bf16[48,896]{1,0:T(8,128)(2,1)S(1)}, bf16[48,896]{1,0:T(8,128)(2,1)S(1)}, u32[]{:S(2)}, u32[]{:S(2)}) %collective-permute-start.7) | collective-permute-done | bytes 86048 | tf_op jit(solution)/shard_map/ppermute | solution.py:454
  61.1 0.9 %collective-permute-done.8.refs_2_ = bf16[48,896]{1,0:T(8,128)(2,1)S(1)} collective-permute-done((bf16[48,896]{1,0:T(8,128)(2,1)S(1)}, bf16[48,896]{1,0:T(8,128)(2,1)S(1)}, u32[]{:S(2)}, u32[]{:S(2)}) %collective-permute-start.8) | collective-permute-done | bytes 86048 | tf_op jit(solution)/shard_map/ppermute | solution.py:454
  62.0 0.7 %owner_sum.1 = (f32[2,48,384]{2,1,0:T(8,128)}, f32[2,48,49]{2,1,0:T(8,128)}) custom-call(f32[48,896]{1,0:T(8,128)S(1)} %get-tuple-element.53.mine_ref, bf16[48,896]{1,0:T(8,128)(2,1)S(1)} %collective-permute-done.6.refs_0_, bf16[48,896]{1,0:T(8,128)(2,1)S(1)} %collective-permute-done.7.refs_1_, bf16[48,896]{1,0:T(8,128)(2,1)S(1)} %collective-permute-done.8.refs_2_), custom_call_target="tpu_custom_call" | custom-call | tf_op jit(solution)/shard_map/owner_sum/pallas_call | solution.py:434
  (3 shorter events, 0.1 us)
Async XLA Ops:
  0.6 6.7 %copy-start.2 = (f32[2,49,384]{2,0,1:T(2,128)S(1)}, f32[2,49,384]{2,0,1:T(2,128)}, u32[]{:S(2)}) copy-start(f32[2,49,384]{2,0,1:T(2,128)} %param.12) | copy-start | bytes 451588
  0.6 6.7 %copy-start.3 = (f32[416,64]{1,0:T(8,128)S(1)}, f32[416,64]{1,0:T(8,128)}, u32[]{:S(2)}) copy-start(f32[416,64]{1,0:T(8,128)} %constant.10.clone.refs_5_) | copy-start | bytes 319492
  5.4 9.7 %collective-permute-start = (bf16[256,384]{1,0:T(8,128)(2,1)S(1)}, bf16[256,384]{1,0:T(8,128)(2,1)S(1)}, u32[]{:S(2)}, u32[]{:S(2)}) collective-permute-start(bf16[256,384]{1,0:T(8,128)(2,1)S(1)} %get-tuple-element.33.refs_1_), channel_id=1, source_target_pairs={{0,8},{8,16},{16,24},{24,32},{32,40},{40,48},{48,56},{56,64},{64,7... | collective-permute-start | bytes 589832 | tf_op jit(solution)/shard_map/ppermute | solution.py:461
  7.4 7.7 %copy-start = (bf16[3,1,8,32,384]{4,3,2,1,0:T(8,128)(2,1)S(1)}, bf16[3,1,8,32,384]{4,3,2,1,0:T(8,128)(2,1)}, u32[]{:S(2)}) copy-start(bf16[3,1,8,32,384]{4,3,2,1,0:T(8,128)(2,1)} %param.10) | copy-start | bytes 1769476
  15.1 10.6 %collective-permute-start.2 = (bf16[256,384]{1,0:T(8,128)(2,1)S(1)}, bf16[256,384]{1,0:T(8,128)(2,1)S(1)}, u32[]{:S(2)}, u32[]{:S(2)}) collective-permute-start(bf16[256,384]{1,0:T(8,128)(2,1)S(1)} %get-tuple-element.39.odd_ref), channel_id=1, source_target_pairs={{8,16},{24,32},{40,48},{56,64},{72,80},{88,96},{104,112},{120,128}... | collective-permute-start | bytes 589832 | tf_op jit(solution)/shard_map/ppermute | solution.py:466
  19.1 6.7 %collective-permute-start.1 = (bf16[256,384]{1,0:T(8,128)(2,1)S(1)}, bf16[256,384]{1,0:T(8,128)(2,1)S(1)}, u32[]{:S(2)}, u32[]{:S(2)}) collective-permute-start(bf16[256,384]{1,0:T(8,128)(2,1)S(1)} %teacher_even.2.refs_1_), channel_id=1, source_target_pairs={{0,8},{16,24},{32,40},{48,56},{64,72},{80,88},{96,104},{112,120},{... | collective-permute-start | bytes 589832 | tf_op jit(solution)/shard_map/ppermute | solution.py:466
  25.9 11.4 %collective-permute-start.4 = (bf16[256,384]{1,0:T(8,128)(2,1)S(1)}, bf16[256,384]{1,0:T(8,128)(2,1)S(1)}, u32[]{:S(2)}, u32[]{:S(2)}) collective-permute-start(bf16[256,384]{1,0:T(8,128)(2,1)S(1)} %get-tuple-element.44.odd_ref), channel_id=1, source_target_pairs={{8,16},{24,32},{40,48},{56,64},{72,80},{88,96},{104,112},{120,128}... | collective-permute-start | bytes 589832 | tf_op jit(solution)/shard_map/ppermute | solution.py:466
  29.8 7.5 %collective-permute-start.3 = (bf16[256,384]{1,0:T(8,128)(2,1)S(1)}, bf16[256,384]{1,0:T(8,128)(2,1)S(1)}, u32[]{:S(2)}, u32[]{:S(2)}) collective-permute-start(bf16[256,384]{1,0:T(8,128)(2,1)S(1)} %teacher_even.3.refs_1_), channel_id=1, source_target_pairs={{0,8},{16,24},{32,40},{48,56},{64,72},{80,88},{96,104},{112,120},{... | collective-permute-start | bytes 589832 | tf_op jit(solution)/shard_map/ppermute | solution.py:466
  37.3 2.9 %copy-start.1 = (bf16[416,64]{1,0:T(8,128)(2,1)S(1)}, bf16[416,64]{1,0:T(8,128)(2,1)}, u32[]{:S(2)}) copy-start(bf16[416,64]{1,0:T(8,128)(2,1)} %constant.11.clone.refs_8_) | copy-start | bytes 159748
  44.1 1.7 %collective-permute-start.5 = (bf16[4,48,896]{2,1,0:T(8,128)(2,1)S(1)}, bf16[4,48,896]{2,1,0:T(8,128)(2,1)S(1)}, u32[]{:S(2)}, u32[]{:S(2)}) collective-permute-start(bf16[4,48,896]{2,1,0:T(8,128)(2,1)S(1)} %get-tuple-element.52), channel_id=1, source_target_pairs={{0,1},{1,0},{2,3},{3,2},{4,5},{5,4},{6,7},{7,6},{8,9},{9,8},{10,11... | collective-permute-start | bytes 1032200 | tf_op jit(solution)/shard_map/ppermute | solution.py:449
  45.9 8.8 %collective-permute-start.6 = (bf16[48,896]{1,0:T(8,128)(2,1)S(1)}, bf16[48,896]{1,0:T(8,128)(2,1)S(1)}, u32[]{:S(2)}, u32[]{:S(2)}) collective-permute-start(bf16[48,896]{1,0:T(8,128)(2,1)S(1)} %get-tuple-element.54), channel_id=1, source_target_pairs={{0,2},{1,3},{2,0},{3,1},{4,6},{5,7},{6,4},{7,5},{8,10},{9,11},{10,... | collective-permute-start | bytes 258056 | tf_op jit(solution)/shard_map/ppermute | solution.py:454
  49.3 11.8 %collective-permute-start.7 = (bf16[48,896]{1,0:T(8,128)(2,1)S(1)}, bf16[48,896]{1,0:T(8,128)(2,1)S(1)}, u32[]{:S(2)}, u32[]{:S(2)}) collective-permute-start(bf16[48,896]{1,0:T(8,128)(2,1)S(1)} %get-tuple-element.55), channel_id=1, source_target_pairs={{0,4},{1,5},{2,6},{3,7},{4,0},{5,1},{6,2},{7,3},{8,12},{9,13},{10,... | collective-permute-start | bytes 258056 | tf_op jit(solution)/shard_map/ppermute | solution.py:454
  54.7 7.3 %collective-permute-start.8 = (bf16[48,896]{1,0:T(8,128)(2,1)S(1)}, bf16[48,896]{1,0:T(8,128)(2,1)S(1)}, u32[]{:S(2)}, u32[]{:S(2)}) collective-permute-start(bf16[48,896]{1,0:T(8,128)(2,1)S(1)} %get-tuple-element.56), channel_id=1, source_target_pairs={{0,6},{1,7},{2,4},{3,5},{4,2},{5,3},{6,0},{7,1},{8,14},{9,15},{10,... | collective-permute-start | bytes 258056 | tf_op jit(solution)/shard_map/ppermute | solution.py:454

commit v3 on v2

--- a/solution.py
+++ b/solution.py
@@ -77,7 +77,7 @@
     return (0.8 * summed).astype(BF16)
 
 
-FLIGHT = 2
+FLIGHT = 3
 MORE = 2
 
 

time: 63.3 us -> 63.3 us (level)
  no operation moved by 1% of the time
where the time goes in v3:
time: 63.3 us; the launch traced here: 62.7 us
  Pallas kernels  29.2 us (46%)
  starting transfers between devices  17.4 us (27%)
  waiting for transfers between devices  15.3 us (24%)
  between operations  0.82 us (1%)
    pallas_call x4, Pallas kernels, student(): pl.pallas_call(functools.partial(student_kernel, first, last), out_shape=...  15.5 us
    ppermute x3, starting transfers between devices, sum_at_owner(): got.append(lax.ppermute(gives[ahead - 1], 'dp', route))  8.77 us
    ppermute x3, waiting for transfers between devices, sum_at_owner(): got.append(lax.ppermute(gives[ahead - 1], 'dp', route))  7.34 us
    ppermute x4, starting transfers between devices, from_parity(): return lax.ppermute(block, axis, [(i, i + 1) for i in devices])  6.53 us
    pallas_call x2, Pallas kernels, even_teacher(): pl.pallas_call(even_teacher_kernel, out_shape=MAP, in_specs=[VMEM] * 3, o...  5.24 us
    pallas_call x1, Pallas kernels, first_teacher(): pl.pallas_call(first_teacher_kernel, out_shape=[MAP, *held], in_specs=[pl...  4.69 us
    ppermute x1, waiting for transfers between devices, from_behind(): lax.ppermute(block, axis, [(i, (i + 1) % devices) for i in range(devices)])  3.31 us
    ppermute x4, waiting for transfers between devices, from_parity(): return lax.ppermute(block, axis, [(i, i + 1) for i in devices])  3.04 us
  transfers between devices with their start and end apart: 9, of which 6 were waited for; matrix products, arithmetic and copies ran while one was open for 0% of the time, Pallas kernels for 27%

profile of v3, /device:TPU:6, one launch (start us, length us, event | category | flops | bytes accessed | tf_op | source)
XLA Modules:
  0.0 62.7 jit_solution(16404955660536316746)
XLA Ops:
  0.6 0.0 copy-start.2
  0.6 0.0 copy-start.3
  0.7 4.7 %teacher.4 = (bf16[256,384]{1,0:T(8,128)(2,1)S(1)}, bf16[6,1152,384]{2,1,0:T(8,128)(2,1)S(1)}, bf16[256,384]{1,0:T(8,128)(2,1)S(1)}, bf16[2,384,384]{2,1,0:T(8,1...) custom-call(bf16[256,384]{1,0:T(8,128)(2,1)} %bitcast.12, bf16[6,1152,384]{2,1,0:T(8,128)(2,1)} %bitcast.11, ...), custom_call_target="tpu_custom_call" | custom-call | flops 1358954496 | bytes 5308416 | tf_op jit(solution)/shard_map/teacher/pallas_call | solution.py:164
  5.4 2.0 %collective-permute-start = (bf16[256,384]{1,0:T(8,128)(2,1)S(1)}, bf16[256,384]{1,0:T(8,128)(2,1)S(1)}, u32[]{:S(2)}, u32[]{:S(2)}) collective-permute-start(bf16[256,384]{1,0:T(8,128)(2,1)S(1)} %get-tuple-element.33.refs_1_), channel_id=1, source_target_pairs={{0,8},{8,16},{16,24},{24,32},{32,40},{40,48},{48,56},{56,64},{64,7... | collective-permute-start | bytes 589832 | tf_op jit(solution)/shard_map/ppermute | solution.py:461
  7.3 0.0 copy-done.2
  7.3 0.0 copy-done.3
  7.4 0.0 copy-start
  7.4 4.4 %student.4 = (f32[2,416,384]{2,1,0:T(8,128)S(1)}, f32[2,384,384]{2,1,0:T(8,128)S(1)}, f32[2,416,384]{2,1,0:T(8,128)S(1)}) custom-call(bf16[256,384]{1,0:T(8,128)(2,1)S(1)} %get-tuple-element.32.refs_0_, bf16[256,384]{1,0:T(8,128)(2,1)S(1)} %get-tuple-element.33.refs_1_, bf16[416,256]{1,0:T(8,128)(2,1)S(1)} %get-tuple-element.34.refs_2_, ...), custom_call_target="tpu_custom_call" | custom-call | flops 981467136 | bytes 8388608 | tf_op jit(solution)/shard_map/student/pallas_call | solution.py:373
  11.8 3.3 %collective-permute-done.refs_0_ = bf16[256,384]{1,0:T(8,128)(2,1)S(1)} collective-permute-done((bf16[256,384]{1,0:T(8,128)(2,1)S(1)}, bf16[256,384]{1,0:T(8,128)(2,1)S(1)}, u32[]{:S(2)}, u32[]{:S(2)}) %collective-permute-start) | collective-permute-done | bytes 196640 | tf_op jit(solution)/shard_map/ppermute | solution.py:461
  15.1 0.0 copy-done
  15.1 1.3 %collective-permute-start.2 = (bf16[256,384]{1,0:T(8,128)(2,1)S(1)}, bf16[256,384]{1,0:T(8,128)(2,1)S(1)}, u32[]{:S(2)}, u32[]{:S(2)}) collective-permute-start(bf16[256,384]{1,0:T(8,128)(2,1)S(1)} %get-tuple-element.39.odd_ref), channel_id=1, source_target_pairs={{8,16},{24,32},{40,48},{56,64},{72,80},{88,96},{104,112},{120,128}... | collective-permute-start | bytes 589832 | tf_op jit(solution)/shard_map/ppermute | solution.py:466
  16.4 2.6 %teacher_even.2.refs_1_ = bf16[256,384]{1,0:T(8,128)(2,1)S(1)} custom-call(bf16[256,384]{1,0:T(8,128)(2,1)S(1)} %get-tuple-element.38.x_ref.refs_0_, bf16[6,1152,384]{2,1,0:T(8,128)(2,1)S(1)} %get-tuple-element.31.w_ref, bf16[256,384]{1,0:T(8,128)(2,1)S(1)} %get-tuple-element.39.odd_ref), custom_call_target="tpu_custom_call" | custom-call | flops 1358954496 | bytes 5308416 | tf_op jit(solution)/shard_map/teacher_even/pallas_call | solution.py:194
  19.0 1.5 %collective-permute-start.1 = (bf16[256,384]{1,0:T(8,128)(2,1)S(1)}, bf16[256,384]{1,0:T(8,128)(2,1)S(1)}, u32[]{:S(2)}, u32[]{:S(2)}) collective-permute-start(bf16[256,384]{1,0:T(8,128)(2,1)S(1)} %teacher_even.2.refs_1_), channel_id=1, source_target_pairs={{0,8},{16,24},{32,40},{48,56},{64,72},{80,88},{96,104},{112,120},{... | collective-permute-start | bytes 589832 | tf_op jit(solution)/shard_map/ppermute | solution.py:466
  20.5 3.6 %student.5 = (f32[2,384,384]{2,1,0:T(8,128)S(1)}, f32[2,416,384]{2,1,0:T(8,128)S(1)}) custom-call(bf16[256,384]{1,0:T(8,128)(2,1)S(1)} %get-tuple-element.38.x_ref.refs_0_, bf16[256,384]{1,0:T(8,128)(2,1)S(1)} %teacher_even.2.refs_1_, bf16[416,256]{1,0:T(8,128)(2,1)S(1)} %get-tuple-element.34.refs_2_, ...), custom_call_target="tpu_custom_call", output_to_operand_aliasing={{0}: (6, {}), {1}: (7, {})} | custom-call | flops 981467136 | bytes 8388608 | tf_op jit(solution)/shard_map/student/pallas_call | solution.py:373
  24.1 1.6 %collective-permute-done.2.x_ref = bf16[256,384]{1,0:T(8,128)(2,1)S(1)} collective-permute-done((bf16[256,384]{1,0:T(8,128)(2,1)S(1)}, bf16[256,384]{1,0:T(8,128)(2,1)S(1)}, u32[]{:S(2)}, u32[]{:S(2)}) %collective-permute-start.2) | collective-permute-done | bytes 196640 | tf_op jit(solution)/shard_map/ppermute | solution.py:466
  25.8 0.0 collective-permute-done.1.refs_0_
  25.8 0.1 teacher.6
  25.8 1.3 %collective-permute-start.4 = (bf16[256,384]{1,0:T(8,128)(2,1)S(1)}, bf16[256,384]{1,0:T(8,128)(2,1)S(1)}, u32[]{:S(2)}, u32[]{:S(2)}) collective-permute-start(bf16[256,384]{1,0:T(8,128)(2,1)S(1)} %get-tuple-element.44.odd_ref), channel_id=1, source_target_pairs={{8,16},{24,32},{40,48},{56,64},{72,80},{88,96},{104,112},{120,128}... | collective-permute-start | bytes 589832 | tf_op jit(solution)/shard_map/ppermute | solution.py:466
  27.1 2.6 %teacher_even.3.refs_1_ = bf16[256,384]{1,0:T(8,128)(2,1)S(1)} custom-call(bf16[256,384]{1,0:T(8,128)(2,1)S(1)} %get-tuple-element.43.x_ref.refs_0_, bf16[6,1152,384]{2,1,0:T(8,128)(2,1)S(1)} %get-tuple-element.31.w_ref, bf16[256,384]{1,0:T(8,128)(2,1)S(1)} %get-tuple-element.44.odd_ref), custom_call_target="tpu_custom_call" | custom-call | flops 1358954496 | bytes 5308416 | tf_op jit(solution)/shard_map/teacher_even/pallas_call | solution.py:194
  29.8 2.5 %collective-permute-start.3 = (bf16[256,384]{1,0:T(8,128)(2,1)S(1)}, bf16[256,384]{1,0:T(8,128)(2,1)S(1)}, u32[]{:S(2)}, u32[]{:S(2)}) collective-permute-start(bf16[256,384]{1,0:T(8,128)(2,1)S(1)} %teacher_even.3.refs_1_), channel_id=1, source_target_pairs={{0,8},{16,24},{32,40},{48,56},{64,72},{80,88},{96,104},{112,120},{... | collective-permute-start | bytes 589832 | tf_op jit(solution)/shard_map/ppermute | solution.py:466
  32.2 3.6 %student.6 = (f32[2,384,384]{2,1,0:T(8,128)S(1)}, f32[2,416,384]{2,1,0:T(8,128)S(1)}) custom-call(bf16[256,384]{1,0:T(8,128)(2,1)S(1)} %get-tuple-element.43.x_ref.refs_0_, bf16[256,384]{1,0:T(8,128)(2,1)S(1)} %teacher_even.3.refs_1_, bf16[416,256]{1,0:T(8,128)(2,1)S(1)} %get-tuple-element.34.refs_2_, ...), custom_call_target="tpu_custom_call", output_to_operand_aliasing={{0}: (6, {}), {1}: (7, {})} | custom-call | flops 981467136 | bytes 8388608 | tf_op jit(solution)/shard_map/student/pallas_call | solution.py:373
  35.8 1.4 %collective-permute-done.4.x_ref = bf16[256,384]{1,0:T(8,128)(2,1)S(1)} collective-permute-done((bf16[256,384]{1,0:T(8,128)(2,1)S(1)}, bf16[256,384]{1,0:T(8,128)(2,1)S(1)}, u32[]{:S(2)}, u32[]{:S(2)}) %collective-permute-start.4) | collective-permute-done | bytes 196640 | tf_op jit(solution)/shard_map/ppermute | solution.py:466
  37.2 0.0 collective-permute-done.3.refs_0_
  37.2 0.0 copy-start.1
  37.3 2.9 %teacher.7 = (bf16[256,384]{1,0:T(8,128)(2,1)S(1)}, bf16[256,384]{1,0:T(8,128)(2,1)S(1)}) custom-call(bf16[3,256,384]{2,1,0:T(8,128)(2,1)S(1)} %bitcast.9, bf16[6,1152,384]{2,1,0:T(8,128)(2,1)S(1)} %get-tuple-element.31.w_ref, f32[2,384,384]{2,1,0:T(8,128)S(1)} %get-tuple-element.46.after.refs_6_, bf16[256,384]{1,0:T(8,128)(2,1)S(1)} %collective-permute-done.3.refs_0_, ...), custom_call_target="tpu_custom_call" | custom-call | flops 1358954496 | bytes 5308416 | tf_op jit(solution)/shard_map/teacher/pallas_call | solution.py:181
  40.1 0.0 copy-done.1
  40.1 3.9 %student.7 = (bf16[4,48,896]{2,1,0:T(8,128)(2,1)S(1)}, bf16[4,48,896]{2,1,0:T(8,128)(2,1)S(1)}, bf16[256,384]{1,0:T(8,128)(2,1)}) custom-call(bf16[256,384]{1,0:T(8,128)(2,1)S(1)} %get-tuple-element.47.refs_0_, bf16[256,384]{1,0:T(8,128)(2,1)S(1)} %get-tuple-element.48.refs_1_, bf16[416,256]{1,0:T(8,128)(2,1)S(1)} %get-tuple-element.34.refs_2_, ...), custom_call_target="tpu_custom_call" | custom-call | flops 981467136 | bytes 8388608 | tf_op jit(solution)/shard_map/student/pallas_call | solution.py:373
  44.1 0.1 collective-permute-start.5
  44.2 1.6 %collective-permute-done.5.got_ref = bf16[4,48,896]{2,1,0:T(8,128)(2,1)S(1)} collective-permute-done((bf16[4,48,896]{2,1,0:T(8,128)(2,1)S(1)}, bf16[4,48,896]{2,1,0:T(8,128)(2,1)S(1)}, u32[]{:S(2)}, u32[]{:S(2)}) %collective-permute-start.5) | collective-permute-done | bytes 344096 | tf_op jit(solution)/shard_map/ppermute | solution.py:449
  45.8 0.1 fold_cores.1
  45.9 3.4 %collective-permute-start.6 = (bf16[48,896]{1,0:T(8,128)(2,1)S(1)}, bf16[48,896]{1,0:T(8,128)(2,1)S(1)}, u32[]{:S(2)}, u32[]{:S(2)}) collective-permute-start(bf16[48,896]{1,0:T(8,128)(2,1)S(1)} %get-tuple-element.54), channel_id=1, source_target_pairs={{0,2},{1,3},{2,0},{3,1},{4,6},{5,7},{6,4},{7,5},{8,10},{9,11},{10,... | collective-permute-start | bytes 258056 | tf_op jit(solution)/shard_map/ppermute | solution.py:454
  49.3 5.4 %collective-permute-start.7 = (bf16[48,896]{1,0:T(8,128)(2,1)S(1)}, bf16[48,896]{1,0:T(8,128)(2,1)S(1)}, u32[]{:S(2)}, u32[]{:S(2)}) collective-permute-start(bf16[48,896]{1,0:T(8,128)(2,1)S(1)} %get-tuple-element.55), channel_id=1, source_target_pairs={{0,4},{1,5},{2,6},{3,7},{4,0},{5,1},{6,2},{7,3},{8,12},{9,13},{10,... | collective-permute-start | bytes 258056 | tf_op jit(solution)/shard_map/ppermute | solution.py:454
  54.7 0.0 collective-permute-start.8
  54.7 0.0 collective-permute-done.6.refs_0_
  54.7 6.5 %collective-permute-done.7.refs_1_ = bf16[48,896]{1,0:T(8,128)(2,1)S(1)} collective-permute-done((bf16[48,896]{1,0:T(8,128)(2,1)S(1)}, bf16[48,896]{1,0:T(8,128)(2,1)S(1)}, u32[]{:S(2)}, u32[]{:S(2)}) %collective-permute-start.7) | collective-permute-done | bytes 86048 | tf_op jit(solution)/shard_map/ppermute | solution.py:454
  61.1 0.9 %collective-permute-done.8.refs_2_ = bf16[48,896]{1,0:T(8,128)(2,1)S(1)} collective-permute-done((bf16[48,896]{1,0:T(8,128)(2,1)S(1)}, bf16[48,896]{1,0:T(8,128)(2,1)S(1)}, u32[]{:S(2)}, u32[]{:S(2)}) %collective-permute-start.8) | collective-permute-done | bytes 86048 | tf_op jit(solution)/shard_map/ppermute | solution.py:454
  62.0 0.7 %owner_sum.1 = (f32[2,48,384]{2,1,0:T(8,128)}, f32[2,48,49]{2,1,0:T(8,128)}) custom-call(f32[48,896]{1,0:T(8,128)S(1)} %get-tuple-element.53.mine_ref, bf16[48,896]{1,0:T(8,128)(2,1)S(1)} %collective-permute-done.6.refs_0_, bf16[48,896]{1,0:T(8,128)(2,1)S(1)} %collective-permute-done.7.refs_1_, bf16[48,896]{1,0:T(8,128)(2,1)S(1)} %collective-permute-done.8.refs_2_), custom_call_target="tpu_custom_call" | custom-call | tf_op jit(solution)/shard_map/owner_sum/pallas_call | solution.py:434
  (3 shorter events, 0.1 us)
Async XLA Ops:
  0.6 6.7 %copy-start.2 = (f32[2,49,384]{2,0,1:T(2,128)S(1)}, f32[2,49,384]{2,0,1:T(2,128)}, u32[]{:S(2)}) copy-start(f32[2,49,384]{2,0,1:T(2,128)} %param.12) | copy-start | bytes 451588
  0.6 6.7 %copy-start.3 = (f32[416,64]{1,0:T(8,128)S(1)}, f32[416,64]{1,0:T(8,128)}, u32[]{:S(2)}) copy-start(f32[416,64]{1,0:T(8,128)} %constant.10.clone.refs_5_) | copy-start | bytes 319492
  5.4 9.7 %collective-permute-start = (bf16[256,384]{1,0:T(8,128)(2,1)S(1)}, bf16[256,384]{1,0:T(8,128)(2,1)S(1)}, u32[]{:S(2)}, u32[]{:S(2)}) collective-permute-start(bf16[256,384]{1,0:T(8,128)(2,1)S(1)} %get-tuple-element.33.refs_1_), channel_id=1, source_target_pairs={{0,8},{8,16},{16,24},{24,32},{32,40},{40,48},{48,56},{56,64},{64,7... | collective-permute-start | bytes 589832 | tf_op jit(solution)/shard_map/ppermute | solution.py:461
  7.4 7.7 %copy-start = (bf16[3,1,8,32,384]{4,3,2,1,0:T(8,128)(2,1)S(1)}, bf16[3,1,8,32,384]{4,3,2,1,0:T(8,128)(2,1)}, u32[]{:S(2)}) copy-start(bf16[3,1,8,32,384]{4,3,2,1,0:T(8,128)(2,1)} %param.10) | copy-start | bytes 1769476
  15.1 10.6 %collective-permute-start.2 = (bf16[256,384]{1,0:T(8,128)(2,1)S(1)}, bf16[256,384]{1,0:T(8,128)(2,1)S(1)}, u32[]{:S(2)}, u32[]{:S(2)}) collective-permute-start(bf16[256,384]{1,0:T(8,128)(2,1)S(1)} %get-tuple-element.39.odd_ref), channel_id=1, source_target_pairs={{8,16},{24,32},{40,48},{56,64},{72,80},{88,96},{104,112},{120,128}... | collective-permute-start | bytes 589832 | tf_op jit(solution)/shard_map/ppermute | solution.py:466
  19.0 6.7 %collective-permute-start.1 = (bf16[256,384]{1,0:T(8,128)(2,1)S(1)}, bf16[256,384]{1,0:T(8,128)(2,1)S(1)}, u32[]{:S(2)}, u32[]{:S(2)}) collective-permute-start(bf16[256,384]{1,0:T(8,128)(2,1)S(1)} %teacher_even.2.refs_1_), channel_id=1, source_target_pairs={{0,8},{16,24},{32,40},{48,56},{64,72},{80,88},{96,104},{112,120},{... | collective-permute-start | bytes 589832 | tf_op jit(solution)/shard_map/ppermute | solution.py:466
  25.8 11.4 %collective-permute-start.4 = (bf16[256,384]{1,0:T(8,128)(2,1)S(1)}, bf16[256,384]{1,0:T(8,128)(2,1)S(1)}, u32[]{:S(2)}, u32[]{:S(2)}) collective-permute-start(bf16[256,384]{1,0:T(8,128)(2,1)S(1)} %get-tuple-element.44.odd_ref), channel_id=1, source_target_pairs={{8,16},{24,32},{40,48},{56,64},{72,80},{88,96},{104,112},{120,128}... | collective-permute-start | bytes 589832 | tf_op jit(solution)/shard_map/ppermute | solution.py:466
  29.8 7.5 %collective-permute-start.3 = (bf16[256,384]{1,0:T(8,128)(2,1)S(1)}, bf16[256,384]{1,0:T(8,128)(2,1)S(1)}, u32[]{:S(2)}, u32[]{:S(2)}) collective-permute-start(bf16[256,384]{1,0:T(8,128)(2,1)S(1)} %teacher_even.3.refs_1_), channel_id=1, source_target_pairs={{0,8},{16,24},{32,40},{48,56},{64,72},{80,88},{96,104},{112,120},{... | collective-permute-start | bytes 589832 | tf_op jit(solution)/shard_map/ppermute | solution.py:466
  37.2 2.9 %copy-start.1 = (bf16[416,64]{1,0:T(8,128)(2,1)S(1)}, bf16[416,64]{1,0:T(8,128)(2,1)}, u32[]{:S(2)}) copy-start(bf16[416,64]{1,0:T(8,128)(2,1)} %constant.11.clone.refs_8_) | copy-start | bytes 159748
  44.1 1.7 %collective-permute-start.5 = (bf16[4,48,896]{2,1,0:T(8,128)(2,1)S(1)}, bf16[4,48,896]{2,1,0:T(8,128)(2,1)S(1)}, u32[]{:S(2)}, u32[]{:S(2)}) collective-permute-start(bf16[4,48,896]{2,1,0:T(8,128)(2,1)S(1)} %get-tuple-element.52), channel_id=1, source_target_pairs={{0,1},{1,0},{2,3},{3,2},{4,5},{5,4},{6,7},{7,6},{8,9},{9,8},{10,11... | collective-permute-start | bytes 1032200 | tf_op jit(solution)/shard_map/ppermute | solution.py:449
  45.9 8.8 %collective-permute-start.6 = (bf16[48,896]{1,0:T(8,128)(2,1)S(1)}, bf16[48,896]{1,0:T(8,128)(2,1)S(1)}, u32[]{:S(2)}, u32[]{:S(2)}) collective-permute-start(bf16[48,896]{1,0:T(8,128)(2,1)S(1)} %get-tuple-element.54), channel_id=1, source_target_pairs={{0,2},{1,3},{2,0},{3,1},{4,6},{5,7},{6,4},{7,5},{8,10},{9,11},{10,... | collective-permute-start | bytes 258056 | tf_op jit(solution)/shard_map/ppermute | solution.py:454
  49.3 11.9 %collective-permute-start.7 = (bf16[48,896]{1,0:T(8,128)(2,1)S(1)}, bf16[48,896]{1,0:T(8,128)(2,1)S(1)}, u32[]{:S(2)}, u32[]{:S(2)}) collective-permute-start(bf16[48,896]{1,0:T(8,128)(2,1)S(1)} %get-tuple-element.55), channel_id=1, source_target_pairs={{0,4},{1,5},{2,6},{3,7},{4,0},{5,1},{6,2},{7,3},{8,12},{9,13},{10,... | collective-permute-start | bytes 258056 | tf_op jit(solution)/shard_map/ppermute | solution.py:454
  54.7 7.3 %collective-permute-start.8 = (bf16[48,896]{1,0:T(8,128)(2,1)S(1)}, bf16[48,896]{1,0:T(8,128)(2,1)S(1)}, u32[]{:S(2)}, u32[]{:S(2)}) collective-permute-start(bf16[48,896]{1,0:T(8,128)(2,1)S(1)} %get-tuple-element.56), channel_id=1, source_target_pairs={{0,6},{1,7},{2,4},{3,5},{4,2},{5,3},{6,0},{7,1},{8,14},{9,15},{10,... | collective-permute-start | bytes 258056 | tf_op jit(solution)/shard_map/ppermute | solution.py:454
